TPU v7x, 256 devices: a whole 4x4x8 slice. The times are simulated.
256 devices in a mesh: row: 32 (over z, y_hi, core), col: 8 (over y_lo, x).
Axes of the slice: x: 4, y: 4 (y_hi: 2, y_lo: 2; y = y_hi * 2 + y_lo), z: 8, core: 2. Of those that a mesh axis runs over, the one named last changes fastest.
Arguments:
- vectors: float32 [8, 131072], P(None, ('row', 'col')), may hold values from -6 to 6
- tiles: float32 [32, 384, 128, 128], P('row', 'col'), may hold values from -0.1875 to 0.1875
- tile_rows: int32 [32, 384], P('row', 'col'), may hold values from 0 to 31
- tile_cols: int32 [32, 384], P('row', 'col'), may hold values from 0 to 31, as said below
- counts: int32 [32, 8], P('row', 'col'), may hold values from 1 to 48, as said below
Outputs:
- product: float32 [8, 131072], P(None, ('row', 'col'))
Inputs may be any that keep to these rules, and one draw needn't show every extreme that they name: `tile_cols`: on grid positions with c = 0 each tile's column is at most its row. `counts`: some grid position holds exactly 48 live tiles.
All inputs are finite; a program needn't handle non-finite values.
Results may differ from a plain program's by a relative error of at most 0.0003.
Values sent between devices are 32-bit elements; how exact they have to be, the bound alone decides.
No kernel may reach another device: no remote copies, remote signals or barrier semaphores. Data moves between devices by JAX's collectives and lax.ppermute only.
A program may use at most 64 MiB of HBM per device.

v0:
```python
import jax
import jax.numpy as jnp
from jax import lax
from jax.sharding import PartitionSpec as P

TILE = 128


def shifted(shard, axis, by):
    size = lax.axis_size(axis)
    return lax.ppermute(shard, axis, [(i, (i + by) % size) for i in range(size)])


def apply_tiles(own_seg, other_seg, tiles, tile_rows, tile_cols, counts):
    width = own_seg.shape[0]
    seg_len = own_seg.shape[1]
    nblocks = seg_len // TILE
    slots = tiles.shape[1]
    tile_set = tiles[0]
    rows_loc = tile_rows[0]
    cols_loc = tile_cols[0]
    live = (jnp.arange(slots, dtype=jnp.int32) < counts[0, 0]).astype(jnp.float32)
    own_blocks = own_seg.reshape(width, nblocks, TILE)
    other_blocks = other_seg.reshape(width, nblocks, TILE)
    positions = jnp.arange(nblocks, dtype=jnp.int32)
    row_hot = (rows_loc[:, None] == positions[None, :]).astype(jnp.float32) * live[:, None]
    col_hot = (cols_loc[:, None] == positions[None, :]).astype(jnp.float32) * live[:, None]
    inbound = jnp.take(other_blocks, cols_loc, axis=1)
    plain = jnp.einsum("ckj,kij->cki", inbound, tile_set, precision=lax.Precision.HIGHEST)
    rowside = jnp.take(own_blocks, rows_loc, axis=1)
    mirror = jnp.einsum("cki,kij->ckj", rowside, tile_set, precision=lax.Precision.HIGHEST)
    row_part = jnp.einsum("cki,kb->cbi", plain, row_hot, precision=lax.Precision.HIGHEST)
    col_part = jnp.einsum("ckj,kb->cbj", mirror, col_hot, precision=lax.Precision.HIGHEST)
    return (row_part.reshape(width, seg_len), col_part.reshape(width, seg_len))


def local(vectors, tiles, tile_rows, tile_cols, counts):
    own_seg = lax.all_gather(vectors, "col", axis=1, tiled=True)
    ncol = lax.axis_size("col")
    width = vectors.shape[0]
    piece_len = vectors.shape[1]
    nearby = [vectors]
    for dist in range(1, ncol):
        nearby.append(shifted(vectors, "row", dist))
    stacked = jnp.stack(nearby, axis=1)
    arrived = lax.all_to_all(stacked, "col", split_axis=1, concat_axis=1, tiled=True)
    other_seg = arrived.reshape(width, ncol * piece_len)
    row_part, col_part = apply_tiles(own_seg, other_seg, tiles, tile_rows, tile_cols, counts)
    split_parts = col_part.reshape(width, ncol, piece_len)
    sorted_parts = lax.all_to_all(split_parts, "col", split_axis=1, concat_axis=1, tiled=True)
    extra = sorted_parts[:, 0, :]
    for dist in range(1, ncol):
        extra = extra + shifted(sorted_parts[:, dist, :], "row", -dist)
    return lax.psum_scatter(row_part, "col", scatter_dimension=1, tiled=True) + extra


def solution(mesh):
    placed = (
        P(None, ("row", "col")),
        P("row", "col", None, None),
        P("row", "col"),
        P("row", "col"),
        P("row", "col"),
    )
    return jax.shard_map(
        local, mesh=mesh, in_specs=placed, out_specs=P(None, ("row", "col")), check_vma=False
    )
```

profile of v0, /device:TPU:32, one launch (start us, length us, event | category | flops | bytes accessed | tf_op | source)
XLA Modules:
  0.0 137.8 jit_solution(2574082718957498377)
XLA Ops:
  6.5 4.5 %collective-permute-start.5 = (f32[8,512]{1,0:T(8,128)}, f32[8,512]{1,0:T(8,128)S(1)}, u32[]{:S(2)}, u32[]{:S(2)}) collective-permute-start(f32[8,512]{1,0:T(8,128)} %param.7), channel_id=1, source_target_pairs={{0,48},{8,56},{16,64},{24,72},{32,80},{40,88},{48,96},{56,104},{64... | collective-permute-start | bytes 49160 | tf_op jit(solution)/shard_map/ppermute | solution.py:11
  11.1 1.1 collective-permute-start.4
  12.2 3.1 %collective-permute-start.3 = (f32[8,512]{1,0:T(8,128)}, f32[8,512]{1,0:T(8,128)S(1)}, u32[]{:S(2)}, u32[]{:S(2)}) collective-permute-start(f32[8,512]{1,0:T(8,128)} %param.7), channel_id=1, source_target_pairs={{0,32},{8,40},{16,48},{24,56},{32,64},{40,72},{48,80},{56,88},{64,... | collective-permute-start | bytes 49160 | tf_op jit(solution)/shard_map/ppermute | solution.py:11
  15.3 3.7 %collective-permute-start.2 = (f32[8,512]{1,0:T(8,128)}, f32[8,512]{1,0:T(8,128)S(1)}, u32[]{:S(2)}, u32[]{:S(2)}) collective-permute-start(f32[8,512]{1,0:T(8,128)} %param.7), channel_id=1, source_target_pairs={{0,24},{8,32},{16,40},{24,48},{32,56},{40,64},{48,72},{56,80},{64,... | collective-permute-start | bytes 49160 | tf_op jit(solution)/shard_map/ppermute | solution.py:11
  19.0 1.2 compare_and_fusion
  20.8 1.3 constant_dynamic-update-slice_fusion.7
  22.1 28.4 %all_gather.3 = f32[8,4096]{1,0:T(8,128)S(1)} all-gather(f32[8,512]{1,0:T(8,128)} %param.7), channel_id=1, replica_groups=mesh['row'=32,'col'=8] {'col'}, dimensions={1}, use_global_device_ids=true | all-gather | bytes 147456 | tf_op jit(solution)/shard_map/all_gather | solution.py:38
  53.1 3.3 %fusion = f32[48,8,128]{2,1,0:T(8,128)S(1)} fusion(f32[1,48,128,128]{3,2,1,0:T(8,128)S(1)} %copy-done, f32[48,8,128]{2,1,0:T(8,128)S(1)} %gather_fusion.1, pred[48]{0:T(512)(128)(4,1)} %compare_and_fusion), kind=kOutput, calls=%fused_computation.2 | convolution fusion | flops 75546624 | bytes 3538992 | tf_op jit(solution)/shard_map/cki,kij->ckj/dot_general | solution.py:31
  57.2 1.8 %collective-permute-start.1 = (f32[8,512]{1,0:T(8,128)S(1)}, f32[8,512]{1,0:T(8,128)S(1)}, u32[]{:S(2)}, u32[]{:S(2)}) collective-permute-start(f32[8,512]{1,0:T(8,128)S(1)} %copy-done.1), channel_id=1, source_target_pairs={{0,16},{8,24},{16,32},{24,40},{32,48},{40,56},{48,64},{56,72},{64,... | collective-permute-start | bytes 49160 | tf_op jit(solution)/shard_map/ppermute | solution.py:11
  59.1 1.3 constant_dynamic-update-slice_fusion.6
  60.4 3.0 %collective-permute-done.1 = f32[8,512]{1,0:T(8,128)S(1)} collective-permute-done((f32[8,512]{1,0:T(8,128)S(1)}, f32[8,512]{1,0:T(8,128)S(1)}, u32[]{:S(2)}, u32[]{:S(2)}) %collective-permute-start.1) | collective-permute-done | bytes 16416 | tf_op jit(solution)/shard_map/ppermute | solution.py:11
  66.4 2.3 %collective-permute-done.6 = f32[8,512]{1,0:T(8,128)S(1)} collective-permute-done((f32[8,512]{1,0:T(8,128)S(1)}, f32[8,512]{1,0:T(8,128)S(1)}, u32[]{:S(2)}, u32[]{:S(2)}) %collective-permute-start.6) | collective-permute-done | bytes 16416 | tf_op jit(solution)/shard_map/ppermute | solution.py:11
  69.3 4.2 %all-to-all-start = ((f32[8,8,512]{2,0,1:T(8,128)}), f32[8,8,512]{2,0,1:T(8,128)S(1)}, u32[]{:S(2)}, u32[]{:S(2)}) async-start(f32[8,8,512]{2,0,1:T(8,128)} %constant_dynamic-update-slice_fusion), calls=%async_computation | async-start | bytes 262144 | tf_op jit(solution)/shard_map/all_to_all | solution.py:46
  74.9 5.2 %all-to-all-done = f32[8,8,512]{2,0,1:T(8,128)S(1)} async-done(((f32[8,8,512]{2,0,1:T(8,128)}), f32[8,8,512]{2,0,1:T(8,128)S(1)}, u32[]{:S(2)}, u32[]{:S(2)}) %all-to-all-start) | async-done | bytes 131104 | tf_op jit(solution)/shard_map/all_to_all | solution.py:46
  80.0 4.0 %all-to-all-start.1 = ((f32[8,8,512]{2,0,1:T(8,128)}), f32[8,8,512]{2,0,1:T(8,128)}, u32[]{:S(2)}, u32[]{:S(2)}) async-start(f32[8,8,512]{2,0,1:T(8,128)} %copy.9), calls=%async_computation.2 | async-start | bytes 262144 | tf_op jit(solution)/shard_map/all_to_all | solution.py:50
  84.9 5.7 %fusion.2 = f32[48,8,128]{2,1,0:T(8,128)S(1)} fusion(f32[1,48,128,128]{3,2,1,0:T(8,128)S(1)} %copy-done, f32[48,8,128]{2,1,0:T(8,128)S(1)} %gather_fusion, pred[48]{0:T(512)(128)(4,1)} %compare_and_fusion.1), kind=kOutput, calls=%fused_computation.4 | convolution fusion | flops 75546624 | bytes 3538992 | tf_op jit(solution)/shard_map/ckj,kij->cki/dot_general | solution.py:29
  90.5 1.0 convolution_bitcast_fusion.1
  93.4 2.9 %collective-permute-start.12 = (f32[8,512]{1,0:T(8,128)S(1)}, f32[8,512]{1,0:T(8,128)S(1)}, u32[]{:S(2)}, u32[]{:S(2)}) collective-permute-start(f32[8,512]{1,0:T(8,128)S(1)} %get-tuple-element.8), channel_id=1, source_target_pairs={{0,208},{8,216},{16,224},{24,232},{32,240},{40,248},{48,0},{56,8},... | collective-permute-start | bytes 49160 | tf_op jit(solution)/shard_map/ppermute | solution.py:11
  96.3 2.9 %collective-permute-start.11 = (f32[8,512]{1,0:T(8,128)S(1)}, f32[8,512]{1,0:T(8,128)S(1)}, u32[]{:S(2)}, u32[]{:S(2)}) collective-permute-start(f32[8,512]{1,0:T(8,128)S(1)} %get-tuple-element.9), channel_id=1, source_target_pairs={{0,216},{8,224},{16,232},{24,240},{32,248},{40,0},{48,8},{56,16},{... | collective-permute-start | bytes 49160 | tf_op jit(solution)/shard_map/ppermute | solution.py:11
  99.2 1.4 %collective-permute-start.10 = (f32[8,512]{1,0:T(8,128)S(1)}, f32[8,512]{1,0:T(8,128)S(1)}, u32[]{:S(2)}, u32[]{:S(2)}) collective-permute-start(f32[8,512]{1,0:T(8,128)S(1)} %get-tuple-element.10), channel_id=1, source_target_pairs={{0,224},{8,232},{16,240},{24,248},{32,0},{40,8},{48,16},{56,24},{6... | collective-permute-start | bytes 49160 | tf_op jit(solution)/shard_map/ppermute | solution.py:11
  100.7 3.1 %collective-permute-start.8 = (f32[8,512]{1,0:T(8,128)S(1)}, f32[8,512]{1,0:T(8,128)S(1)}, u32[]{:S(2)}, u32[]{:S(2)}) collective-permute-start(f32[8,512]{1,0:T(8,128)S(1)} %get-tuple-element.12), channel_id=1, source_target_pairs={{0,240},{8,248},{16,0},{24,8},{32,16},{40,24},{48,32},{56,40},{64,... | collective-permute-start | bytes 49160 | tf_op jit(solution)/shard_map/ppermute | solution.py:11
  103.7 1.6 %collective-permute-done.9 = f32[8,512]{1,0:T(8,128)S(1)} collective-permute-done((f32[8,512]{1,0:T(8,128)S(1)}, f32[8,512]{1,0:T(8,128)S(1)}, u32[]{:S(2)}, u32[]{:S(2)}) %collective-permute-start.9) | collective-permute-done | bytes 16416 | tf_op jit(solution)/shard_map/ppermute | solution.py:11
  106.0 23.7 %reduce-scatter.2.cloned.1.call-done = f32[8,512]{1,0:T(8,128)} async-done(((f32[8,4096]{1,0:T(8,128)}), f32[8,512]{1,0:T(8,128)}) %reduce-scatter.2.cloned.1.call-update) | async-done | bytes 16400 | tf_op jit(solution)/shard_map/reduce_scatter | solution.py:54
  129.6 1.4 fusion.23
  (46 shorter events, 11.8 us)
Async XLA Ops:
  6.5 46.5 %copy-start = (f32[1,48,128,128]{3,2,1,0:T(8,128)S(1)}, f32[1,48,128,128]{3,2,1,0:T(8,128)}, u32[]{:S(2)}) copy-start(f32[1,48,128,128]{3,2,1,0:T(8,128)} %param.8) | copy-start | bytes 9437188
  6.5 50.7 %copy-start.1 = (f32[8,512]{1,0:T(8,128)S(1)}, f32[8,512]{1,0:T(8,128)}, u32[]{:S(2)}) copy-start(f32[8,512]{1,0:T(8,128)} %param.7) | copy-start | bytes 49156
  6.5 59.3 %collective-permute-start.5 = (f32[8,512]{1,0:T(8,128)}, f32[8,512]{1,0:T(8,128)S(1)}, u32[]{:S(2)}, u32[]{:S(2)}) collective-permute-start(f32[8,512]{1,0:T(8,128)} %param.7), channel_id=1, source_target_pairs={{0,48},{8,56},{16,64},{24,72},{32,80},{40,88},{48,96},{56,104},{64... | collective-permute-start | bytes 49160 | tf_op jit(solution)/shard_map/ppermute | solution.py:11
  11.1 54.1 %collective-permute-start.4 = (f32[8,512]{1,0:T(8,128)}, f32[8,512]{1,0:T(8,128)S(1)}, u32[]{:S(2)}, u32[]{:S(2)}) collective-permute-start(f32[8,512]{1,0:T(8,128)} %param.7), channel_id=1, source_target_pairs={{0,40},{8,48},{16,56},{24,64},{32,72},{40,80},{48,88},{56,96},{64,... | collective-permute-start | bytes 49160 | tf_op jit(solution)/shard_map/ppermute | solution.py:11
  12.2 52.4 %collective-permute-start.3 = (f32[8,512]{1,0:T(8,128)}, f32[8,512]{1,0:T(8,128)S(1)}, u32[]{:S(2)}, u32[]{:S(2)}) collective-permute-start(f32[8,512]{1,0:T(8,128)} %param.7), channel_id=1, source_target_pairs={{0,32},{8,40},{16,48},{24,56},{32,64},{40,72},{48,80},{56,88},{64,... | collective-permute-start | bytes 49160 | tf_op jit(solution)/shard_map/ppermute | solution.py:11
  15.3 48.7 %collective-permute-start.2 = (f32[8,512]{1,0:T(8,128)}, f32[8,512]{1,0:T(8,128)S(1)}, u32[]{:S(2)}, u32[]{:S(2)}) collective-permute-start(f32[8,512]{1,0:T(8,128)} %param.7), channel_id=1, source_target_pairs={{0,24},{8,32},{16,40},{24,48},{32,56},{40,64},{48,72},{56,80},{64,... | collective-permute-start | bytes 49160 | tf_op jit(solution)/shard_map/ppermute | solution.py:11
  19.0 38.2 %collective-permute-start = (f32[8,512]{1,0:T(8,128)}, f32[8,512]{1,0:T(8,128)}, u32[]{:S(2)}, u32[]{:S(2)}) collective-permute-start(f32[8,512]{1,0:T(8,128)} %param.7), channel_id=1, source_target_pairs={{0,8},{8,16},{16,24},{24,32},{32,40},{40,48},{48,56},{56,64},{64,7... | collective-permute-start | bytes 49160 | tf_op jit(solution)/shard_map/ppermute | solution.py:11
  53.1 3.4 %copy-start.2 = (f32[48]{0:T(128)S(1)}, f32[48]{0:T(128)}, u32[]{:S(2)}) copy-start(f32[48]{0:T(128)} %compare_convert_fusion) | copy-start | bytes 580
  53.1 3.4 %copy-start.3 = (s32[1,48]{1,0:T(1,128)S(1)}, s32[1,48]{1,0:T(1,128)}, u32[]{:S(2)}) copy-start(s32[1,48]{1,0:T(1,128)} %param.10) | copy-start | bytes 580
  57.2 6.1 %collective-permute-start.1 = (f32[8,512]{1,0:T(8,128)S(1)}, f32[8,512]{1,0:T(8,128)S(1)}, u32[]{:S(2)}, u32[]{:S(2)}) collective-permute-start(f32[8,512]{1,0:T(8,128)S(1)} %copy-done.1), channel_id=1, source_target_pairs={{0,16},{8,24},{16,32},{24,40},{32,48},{40,56},{48,64},{56,72},{64,... | collective-permute-start | bytes 49160 | tf_op jit(solution)/shard_map/ppermute | solution.py:11
  63.4 5.3 %collective-permute-start.6 = (f32[8,512]{1,0:T(8,128)S(1)}, f32[8,512]{1,0:T(8,128)S(1)}, u32[]{:S(2)}, u32[]{:S(2)}) collective-permute-start(f32[8,512]{1,0:T(8,128)S(1)} %copy-done.1), channel_id=1, source_target_pairs={{0,56},{8,64},{16,72},{24,80},{32,88},{40,96},{48,104},{56,112},{6... | collective-permute-start | bytes 49160 | tf_op jit(solution)/shard_map/ppermute | solution.py:11
  69.3 10.8 %all-to-all-start = ((f32[8,8,512]{2,0,1:T(8,128)}), f32[8,8,512]{2,0,1:T(8,128)S(1)}, u32[]{:S(2)}, u32[]{:S(2)}) async-start(f32[8,8,512]{2,0,1:T(8,128)} %constant_dynamic-update-slice_fusion), calls=%async_computation | async-start | bytes 262144 | tf_op jit(solution)/shard_map/all_to_all | solution.py:46
  80.0 12.2 %all-to-all-start.1 = ((f32[8,8,512]{2,0,1:T(8,128)}), f32[8,8,512]{2,0,1:T(8,128)}, u32[]{:S(2)}, u32[]{:S(2)}) async-start(f32[8,8,512]{2,0,1:T(8,128)} %copy.9), calls=%async_computation.2 | async-start | bytes 262144 | tf_op jit(solution)/shard_map/all_to_all | solution.py:50
  84.0 45.6 %reduce-scatter.2.cloned.1.call-start = ((), (), s32[]{:S(2)}) async-start(), calls=%async_computation.3 | async-start | bytes 147456 | tf_op jit(solution)/shard_map/reduce_scatter | solution.py:54
  93.1 7.6 %collective-permute-start.7 = (f32[8,512]{1,0:T(8,128)S(1)}, f32[8,512]{1,0:T(8,128)S(1)}, u32[]{:S(2)}, u32[]{:S(2)}) collective-permute-start(f32[8,512]{1,0:T(8,128)S(1)} %get-tuple-element.6), channel_id=1, source_target_pairs={{0,248},{8,0},{16,8},{24,16},{32,24},{40,32},{48,40},{56,48},{64,5... | collective-permute-start | bytes 49160 | tf_op jit(solution)/shard_map/ppermute | solution.py:11
  93.2 7.5 %collective-permute-start.13 = (f32[8,512]{1,0:T(8,128)S(1)}, f32[8,512]{1,0:T(8,128)S(1)}, u32[]{:S(2)}, u32[]{:S(2)}) collective-permute-start(f32[8,512]{1,0:T(8,128)S(1)} %get-tuple-element.7), channel_id=1, source_target_pairs={{0,200},{8,208},{16,216},{24,224},{32,232},{40,240},{48,248},{56,0... | collective-permute-start | bytes 49160 | tf_op jit(solution)/shard_map/ppermute | solution.py:11
  93.4 10.3 %collective-permute-start.12 = (f32[8,512]{1,0:T(8,128)S(1)}, f32[8,512]{1,0:T(8,128)S(1)}, u32[]{:S(2)}, u32[]{:S(2)}) collective-permute-start(f32[8,512]{1,0:T(8,128)S(1)} %get-tuple-element.8), channel_id=1, source_target_pairs={{0,208},{8,216},{16,224},{24,232},{32,240},{40,248},{48,0},{56,8},... | collective-permute-start | bytes 49160 | tf_op jit(solution)/shard_map/ppermute | solution.py:11
  96.3 7.4 %collective-permute-start.11 = (f32[8,512]{1,0:T(8,128)S(1)}, f32[8,512]{1,0:T(8,128)S(1)}, u32[]{:S(2)}, u32[]{:S(2)}) collective-permute-start(f32[8,512]{1,0:T(8,128)S(1)} %get-tuple-element.9), channel_id=1, source_target_pairs={{0,216},{8,224},{16,232},{24,240},{32,248},{40,0},{48,8},{56,16},{... | collective-permute-start | bytes 49160 | tf_op jit(solution)/shard_map/ppermute | solution.py:11
  99.2 4.5 %collective-permute-start.10 = (f32[8,512]{1,0:T(8,128)S(1)}, f32[8,512]{1,0:T(8,128)S(1)}, u32[]{:S(2)}, u32[]{:S(2)}) collective-permute-start(f32[8,512]{1,0:T(8,128)S(1)} %get-tuple-element.10), channel_id=1, source_target_pairs={{0,224},{8,232},{16,240},{24,248},{32,0},{40,8},{48,16},{56,24},{6... | collective-permute-start | bytes 49160 | tf_op jit(solution)/shard_map/ppermute | solution.py:11
  100.6 4.7 %collective-permute-start.9 = (f32[8,512]{1,0:T(8,128)S(1)}, f32[8,512]{1,0:T(8,128)S(1)}, u32[]{:S(2)}, u32[]{:S(2)}) collective-permute-start(f32[8,512]{1,0:T(8,128)S(1)} %get-tuple-element.11), channel_id=1, source_target_pairs={{0,232},{8,240},{16,248},{24,0},{32,8},{40,16},{48,24},{56,32},{64... | collective-permute-start | bytes 49160 | tf_op jit(solution)/shard_map/ppermute | solution.py:11
  100.7 5.3 %collective-permute-start.8 = (f32[8,512]{1,0:T(8,128)S(1)}, f32[8,512]{1,0:T(8,128)S(1)}, u32[]{:S(2)}, u32[]{:S(2)}) collective-permute-start(f32[8,512]{1,0:T(8,128)S(1)} %get-tuple-element.12), channel_id=1, source_target_pairs={{0,240},{8,248},{16,0},{24,8},{32,16},{40,24},{48,32},{56,40},{64,... | collective-permute-start | bytes 49160 | tf_op jit(solution)/shard_map/ppermute | solution.py:11
Sparse Core Ops, SparseCore 0:
  92.4 37.2 reduce-scatter.1
where the time goes:
time: 139 us; the launch traced here: 138 us
  waiting for transfers between devices  36.3 us (26%)
  starting transfers between devices  33.3 us (24%)
  blocking collectives  28.4 us (20%)
  between operations  14.2 us (10%)
  matrix products  10.3 us (7%)
  local copies, waits for them, and re-layouts  9.89 us (7%)
  other arithmetic  5.47 us (4%)
    all_gather x1, blocking collectives, local(): own_seg = lax.all_gather(vectors, 'col', axis=1, tiled=True)  28.4 us
    ppermute x14, starting transfers between devices, shifted(): lax.ppermute(shard, axis, [(i, (i + by) % size) for i in range(size)])  24.9 us
    reduce_scatter x1, waiting for transfers between devices, local(): lax.psum_scatter(row_part, 'col', scatter_dimension=1, tiled=True) + extra  23.7 us
    ppermute x14, waiting for transfers between devices, shifted(): lax.ppermute(shard, axis, [(i, (i + by) % size) for i in range(size)])  7.5 us
    unnamed x16, local copies, waits for them, and re-layouts  6.37 us
    dot_general x1, matrix products, apply_tiles(): jnp.einsum('ckj,kij->cki', inbound, tile_set, precision=lax.Precision.HIG...  5.66 us
    all_to_all x1, waiting for transfers between devices, local(): lax.all_to_all(stacked, 'col', split_axis=1, concat_axis=1, tiled=True)  5.16 us
    all_to_all x1, starting transfers between devices, local(): lax.all_to_all(stacked, 'col', split_axis=1, concat_axis=1, tiled=True)  4.17 us
  transfers between devices with their start and end apart: 17, of which 6 were waited for; matrix products, arithmetic and copies ran while one was open for 17% of the time, Pallas kernels for 0%

commit v1 on v0

v1 whole, which is shorter than its diff:
```python
import functools

import jax
import jax.numpy as jnp
from jax import lax
from jax.experimental import pallas as pl
from jax.experimental.pallas import tpu as pltpu
from jax.sharding import PartitionSpec as P

TILE = 128
AXES = ("row", "col")


def split(x):
    hi = x.astype(jnp.bfloat16)
    return hi, x - hi.astype(jnp.float32)


def tiles_kernel(transposed, count_ref, from_ref, to_ref, seg_ref, tiles_ref, out_ref):
    slots = tiles_ref.shape[1]
    width = seg_ref.shape[1]
    dims = (((1,), (1 if transposed else 0,)), ((), ()))
    out_ref[...] = jnp.zeros_like(out_ref)
    for t in range(slots):
        live = t < count_ref[0, 0]
        vec = jnp.where(live, seg_ref[from_ref[0, t]], 0.0)
        vec_hi, vec_lo = split(vec)
        both = jnp.concatenate([vec_hi.astype(jnp.float32), vec_lo], axis=0).astype(jnp.bfloat16)
        tile_hi, tile_lo = split(tiles_ref[0, t])
        main = lax.dot_general(both, tile_hi, dims, preferred_element_type=jnp.float32)
        rest = lax.dot_general(both, tile_lo.astype(jnp.bfloat16), dims, preferred_element_type=jnp.float32)
        to = to_ref[0, t]
        out_ref[to] = out_ref[to] + (main[:width] + (main[width:] + rest[:width]))


def apply_tiles(transposed, seg, tiles, come_from, go_to, counts):
    smem = pl.BlockSpec(memory_space=pltpu.SMEM)
    vmem = pl.BlockSpec(memory_space=pltpu.VMEM)
    slots = tiles.shape[1]
    return pl.pallas_call(
        functools.partial(tiles_kernel, transposed),
        out_shape=jax.ShapeDtypeStruct(seg.shape, jnp.float32),
        in_specs=[smem, smem, smem, vmem, vmem],
        out_specs=vmem,
        compiler_params=pltpu.CompilerParams(vmem_limit_bytes=32 * 2**20),
        cost_estimate=pl.CostEstimate(
            flops=2 * 4 * slots * 8 * TILE * TILE, bytes_accessed=slots * TILE * TILE * 4, transcendentals=0
        ),
    )(counts, come_from, go_to, seg, tiles)


def local(vectors, tiles, tile_rows, tile_cols, counts):
    nrow, ncol = lax.axis_size("row"), lax.axis_size("col")
    width, piece_len = vectors.shape
    per = piece_len // TILE

    def place(r, c):
        return (r % nrow) * ncol + c

    onward = [(place(r, c), place(r + c, c)) for r in range(nrow) for c in range(ncol)]
    piece = vectors.reshape(width, per, TILE).transpose(1, 0, 2)
    own = lax.all_to_all(
        jnp.broadcast_to(piece[None], (ncol, per, width, TILE)), "col", split_axis=0, concat_axis=0, tiled=True
    )
    own_seg = own.reshape(ncol * per, width, TILE)
    other_seg = lax.ppermute(own_seg, AXES, onward)
    col_part = apply_tiles(False, own_seg, tiles, tile_rows, tile_cols, counts)
    home = lax.ppermute(col_part, AXES, [(b, a) for a, b in onward])
    row_part = apply_tiles(True, other_seg, tiles, tile_cols, tile_rows, counts)
    total = (row_part + home).reshape(ncol, per, width, TILE)
    parts = lax.all_to_all(total, "col", split_axis=0, concat_axis=0, tiled=True)
    return parts.sum(axis=0).transpose(1, 0, 2).reshape(width, piece_len)


def solution(mesh):
    placed = (
        P(None, AXES),
        P("row", "col", None, None),
        P("row", "col"),
        P("row", "col"),
        P("row", "col"),
    )
    return jax.shard_map(local, mesh=mesh, in_specs=placed, out_specs=P(None, AXES), check_vma=False)
```

time: 139 us -> 47.8 us (0.34)
  the two profiles are of different devices: /device:TPU:32 before, /device:TPU:80 now
where the time goes in v1:
time: 47.8 us; the launch traced here: 47.4 us
  blocking collectives  25.4 us (53%)
  starting transfers between devices  6.35 us (13%)
  waiting for transfers between devices  5.94 us (12%)
  local copies, waits for them, and re-layouts  4.57 us (10%)
  Pallas kernels  3.73 us (8%)
  between operations  0.74 us (2%)
  other arithmetic  0.64 us (1%)
    all_to_all x1, blocking collectives, local(): lax.all_to_all(total, 'col', split_axis=0, concat_axis=0, tiled=True)  25.4 us
    all_to_all x1, waiting for transfers between devices, local(): lax.all_to_all(jnp.broadcast_to(piece[None], (ncol, per, width, TILE)), '...  5.93 us
    all_to_all x1, starting transfers between devices, local(): lax.all_to_all(jnp.broadcast_to(piece[None], (ncol, per, width, TILE)), '...  5.02 us
    pallas_call x2, Pallas kernels, apply_tiles(): pl.pallas_call(functools.partial(tiles_kernel, transposed), out_shape=jax...  3.73 us
    unnamed x8, local copies, waits for them, and re-layouts  3.2 us
    broadcast_in_dim x1, local copies, waits for them, and re-layouts, local(): jnp.broadcast_to(piece[None], (ncol, per, width, TILE))  1.37 us
  transfers between devices with their start and end apart: 3, of which 1 were waited for; matrix products, arithmetic and copies ran while one was open for 0% of the time, Pallas kernels for 8%

profile of v1, /device:TPU:80, one launch (start us, length us, event | category | flops | bytes accessed | tf_op | source)
XLA Modules:
  0.0 47.4 jit_solution(15819306422751777168)
XLA Ops:
  0.0 1.4 %broadcast_in_dim.2 = f32[8,4,8,128]{3,2,1,0:T(8,128)} broadcast(f32[4,8,128]{2,1,0:T(8,128)} %bitcast.11), dimensions={1,2,3} | broadcast | bytes 147456 | tf_op jit(solution)/shard_map/broadcast_in_dim | solution.py:63
  1.4 5.0 %all-to-all-start = ((f32[8,4,8,128]{3,2,1,0:T(8,128)}), f32[8,4,8,128]{3,2,1,0:T(8,128)S(1)}, u32[]{:S(2)}, u32[]{:S(2)}) async-start(f32[8,4,8,128]{3,2,1,0:T(8,128)} %broadcast_in_dim.2), calls=%async_computation | async-start | bytes 262144 | tf_op jit(solution)/shard_map/all_to_all | solution.py:62
  7.0 5.9 %all-to-all-done = f32[8,4,8,128]{3,2,1,0:T(8,128)S(1)} async-done(((f32[8,4,8,128]{3,2,1,0:T(8,128)}), f32[8,4,8,128]{3,2,1,0:T(8,128)S(1)}, u32[]{:S(2)}, u32[]{:S(2)}) %all-to-all-start) | async-done | bytes 131104 | tf_op jit(solution)/shard_map/all_to_all | solution.py:62
  13.0 0.7 %collective-permute-start = (f32[32,8,128]{2,1,0:T(8,128)S(1)}, f32[32,8,128]{2,1,0:T(8,128)S(1)}, u32[]{:S(2)}, u32[]{:S(2)}) collective-permute-start(f32[32,8,128]{2,1,0:T(8,128)S(1)} %bitcast.8), channel_id=1, source_target_pairs={{0,0},{1,9},{2,18},{3,27},{4,36},{5,45},{6,54},{7,63},{8,8},{9,17}... | collective-permute-start | bytes 393224 | tf_op jit(solution)/shard_map/ppermute | solution.py:66
  13.6 0.0 copy-start
  13.7 1.9 %copy-done = f32[1,48,128,128]{3,2,1,0:T(8,128)S(1)} copy-done((f32[1,48,128,128]{3,2,1,0:T(8,128)S(1)}, f32[1,48,128,128]{3,2,1,0:T(8,128)}, u32[]{:S(2)}) %copy-start) | copy-done | bytes 3145752
  15.5 0.0 copy-start.2
  15.5 0.7 %copy-done.2 = s32[1,48]{1,0:T(1,128)S(1)} copy-done((s32[1,48]{1,0:T(1,128)S(1)}, s32[1,48]{1,0:T(1,128)}, u32[]{:S(2)}) %copy-start.2) | copy-done | bytes 216
  16.2 0.0 copy-start.3
  16.2 0.7 %copy-done.3 = s32[1,48]{1,0:T(1,128)S(1)} copy-done((s32[1,48]{1,0:T(1,128)S(1)}, s32[1,48]{1,0:T(1,128)}, u32[]{:S(2)}) %copy-start.3) | copy-done | bytes 216
  16.8 0.0 copy-start.1
  16.8 1.5 %shard_map.56 = f32[32,8,128]{2,1,0:T(8,128)S(1)} custom-call(s32[1,1]{1,0:T(1,128)S(6)} %copy.6.count_ref, s32[1,48]{1,0:T(1,128)S(1)} %copy-done.3, s32[1,48]{1,0:T(1,128)S(1)} %copy-done.2, f32[32,8,128]{2,1,0:T(8,128)S(1)} %bitcast.9, f32[1,48,128,128]{3,2,1,0:T(8,128)S(1)} %copy-done), custom_call_target="tpu_custom_call" | custom-call | flops 50331648 | bytes 3145728 | tf_op jit(solution)/shard_map/pallas_call | solution.py:40
  18.3 0.7 %collective-permute-start.1 = (f32[32,8,128]{2,1,0:T(8,128)S(1)}, f32[32,8,128]{2,1,0:T(8,128)S(1)}, u32[]{:S(2)}, u32[]{:S(2)}) collective-permute-start(f32[32,8,128]{2,1,0:T(8,128)S(1)} %shard_map.56), channel_id=1, source_target_pairs={{0,0},{9,1},{18,2},{27,3},{36,4},{45,5},{54,6},{63,7},{8,8},{17,9}... | collective-permute-start | bytes 393224 | tf_op jit(solution)/shard_map/ppermute | solution.py:68
  19.0 0.0 collective-permute-done.seg_ref
  19.0 0.0 copy-done.1
  19.0 2.3 %shard_map.55 = f32[32,8,128]{2,1,0:T(8,128)S(1)} custom-call(s32[1,1]{1,0:T(1,128)S(6)} %copy.6.count_ref, s32[1,48]{1,0:T(1,128)S(1)} %copy-done.2, s32[1,48]{1,0:T(1,128)S(1)} %copy-done.3, f32[32,8,128]{2,1,0:T(8,128)S(1)} %collective-permute-done.seg_ref, f32[1,48,128,128]{3,2,1,0:T(8,128)S(1)} %copy-done.1), custom_call_target="tpu_custom_call" | custom-call | flops 50331648 | bytes 3145728 | tf_op jit(solution)/shard_map/pallas_call | solution.py:40
  21.3 0.0 collective-permute-done.1
  21.3 25.4 %all_to_all.10 = f32[8,4,8,128]{3,2,1,0:T(8,128)S(1)} all-to-all(f32[8,4,8,128]{3,2,1,0:T(8,128)S(1)} %bitcast.10), channel_id=1, replica_groups=mesh['row'=32,'col'=8] {'col'}, dimensions={0} | all-to-all | bytes 262144 | tf_op jit(solution)/shard_map/all_to_all | solution.py:71
  46.7 0.6 %reduce_sum.9 = f32[4,8,128]{2,1,0:T(8,128)} reduce(f32[8,4,8,128]{3,2,1,0:T(8,128)S(1)} %all_to_all.10, f32[]{:T(128)} %constant.0.clone.1), dimensions={0}, to_apply=%region_0.0 | reduce | flops 28672 | bytes 147460 | tf_op jit(solution)/shard_map/reduce_sum | solution.py:72
  (1 shorter events, 0.0 us)
Async XLA Ops:
  1.4 11.6 %all-to-all-start = ((f32[8,4,8,128]{3,2,1,0:T(8,128)}), f32[8,4,8,128]{3,2,1,0:T(8,128)S(1)}, u32[]{:S(2)}, u32[]{:S(2)}) async-start(f32[8,4,8,128]{3,2,1,0:T(8,128)} %broadcast_in_dim.2), calls=%async_computation | async-start | bytes 262144 | tf_op jit(solution)/shard_map/all_to_all | solution.py:62
  13.0 6.0 %collective-permute-start = (f32[32,8,128]{2,1,0:T(8,128)S(1)}, f32[32,8,128]{2,1,0:T(8,128)S(1)}, u32[]{:S(2)}, u32[]{:S(2)}) collective-permute-start(f32[32,8,128]{2,1,0:T(8,128)S(1)} %bitcast.8), channel_id=1, source_target_pairs={{0,0},{1,9},{2,18},{3,27},{4,36},{5,45},{6,54},{7,63},{8,8},{9,17}... | collective-permute-start | bytes 393224 | tf_op jit(solution)/shard_map/ppermute | solution.py:66
  13.6 1.9 %copy-start = (f32[1,48,128,128]{3,2,1,0:T(8,128)S(1)}, f32[1,48,128,128]{3,2,1,0:T(8,128)}, u32[]{:S(2)}) copy-start(f32[1,48,128,128]{3,2,1,0:T(8,128)} %tiles_ref.3) | copy-start | bytes 9437188
  15.5 0.7 %copy-start.2 = (s32[1,48]{1,0:T(1,128)S(1)}, s32[1,48]{1,0:T(1,128)}, u32[]{:S(2)}) copy-start(s32[1,48]{1,0:T(1,128)} %to_ref.3) | copy-start | bytes 580
  16.2 0.7 %copy-start.3 = (s32[1,48]{1,0:T(1,128)S(1)}, s32[1,48]{1,0:T(1,128)}, u32[]{:S(2)}) copy-start(s32[1,48]{1,0:T(1,128)} %from_ref.3) | copy-start | bytes 580
  16.8 2.2 %copy-start.1 = (f32[1,48,128,128]{3,2,1,0:T(8,128)S(1)}, f32[1,48,128,128]{3,2,1,0:T(8,128)}, u32[]{:S(2)}) copy-start(f32[1,48,128,128]{3,2,1,0:T(8,128)} %tiles_ref.3) | copy-start | bytes 9437188
  18.3 3.0 %collective-permute-start.1 = (f32[32,8,128]{2,1,0:T(8,128)S(1)}, f32[32,8,128]{2,1,0:T(8,128)S(1)}, u32[]{:S(2)}, u32[]{:S(2)}) collective-permute-start(f32[32,8,128]{2,1,0:T(8,128)S(1)} %shard_map.56), channel_id=1, source_target_pairs={{0,0},{9,1},{18,2},{27,3},{36,4},{45,5},{54,6},{63,7},{8,8},{17,9}... | collective-permute-start | bytes 393224 | tf_op jit(solution)/shard_map/ppermute | solution.py:68

commit v2 on v1

v2 whole, which is shorter than its diff:
```python
import functools

import jax
import jax.numpy as jnp
from jax import lax
from jax.experimental import pallas as pl
from jax.experimental.pallas import tpu as pltpu
from jax.sharding import PartitionSpec as P

TILE = 128
AXES = ("row", "col")
SMEM = pl.BlockSpec(memory_space=pltpu.SMEM)
VMEM = pl.BlockSpec(memory_space=pltpu.VMEM)


def split(x):
    hi = x.astype(jnp.bfloat16)
    return hi, (x - hi.astype(jnp.float32)).astype(jnp.bfloat16)


def stage_kernel(*refs):
    vec_ref, *sources = refs[:5]
    copies_ref, *targets = refs[5:10]
    sems = refs[10]
    ncol = copies_ref.shape[0]
    moves = [pltpu.make_async_copy(vec_ref, copies_ref.at[k], sems.at[k]) for k in range(ncol)]
    moves += [
        pltpu.make_async_copy(s, t, sems.at[ncol + n]) for n, (s, t) in enumerate(zip(sources, targets, strict=True))
    ]
    for move in moves:
        move.start()
    for move in moves:
        move.wait()


def stage(vectors, tiles, tile_rows, tile_cols, counts, ncol):
    rest = [tiles, tile_rows, tile_cols, counts]
    return pl.pallas_call(
        stage_kernel,
        out_shape=[pltpu.VMEM((ncol, *vectors.shape), vectors.dtype), pltpu.VMEM(tiles.shape, tiles.dtype)]
        + [pltpu.SMEM(a.shape, a.dtype) for a in rest[1:]],
        in_specs=[pl.BlockSpec(memory_space=pltpu.HBM)] * 5,
        out_specs=[VMEM, VMEM, SMEM, SMEM, SMEM],
        scratch_shapes=[pltpu.SemaphoreType.DMA((ncol + 4,))],
        cost_estimate=pl.CostEstimate(flops=0, bytes_accessed=tiles.size * 4, transcendentals=0),
    )(vectors, *rest)


def tiles_kernel(mirrored, count_ref, rows_ref, cols_ref, seg_ref, tiles_ref, out_ref):
    slots = tiles_ref.shape[1]
    width = seg_ref.shape[1]
    dims = (((1,), (0 if mirrored else 1,)), ((), ()))
    out_ref[...] = jnp.zeros_like(out_ref)
    for t in range(slots):
        row, col = rows_ref[0, t], cols_ref[0, t]
        vec = jnp.where(t < count_ref[0, 0], seg_ref[row if mirrored else col], 0.0)
        hi = vec.astype(jnp.bfloat16).astype(jnp.float32)
        both = jnp.concatenate([hi, vec - hi], axis=0).astype(jnp.bfloat16)
        tile_hi, tile_lo = split(tiles_ref[0, t])
        main = lax.dot_general(both, tile_hi, dims, preferred_element_type=jnp.float32)
        rest = lax.dot_general(both, tile_lo, dims, preferred_element_type=jnp.float32)
        to = col if mirrored else row
        out_ref[to] = out_ref[to] + (main[:width] + (main[width:] + rest[:width]))


def apply_tiles(mirrored, seg, tiles, tile_rows, tile_cols, counts):
    slots = tiles.shape[1]
    return pl.pallas_call(
        functools.partial(tiles_kernel, mirrored),
        out_shape=jax.ShapeDtypeStruct(seg.shape, jnp.float32),
        in_specs=[SMEM, SMEM, SMEM, VMEM, VMEM],
        out_specs=VMEM,
        compiler_params=pltpu.CompilerParams(vmem_limit_bytes=32 * 2**20),
        cost_estimate=pl.CostEstimate(
            flops=2 * 4 * slots * 8 * TILE * TILE, bytes_accessed=slots * TILE * TILE * 4, transcendentals=0
        ),
    )(counts, tile_rows, tile_cols, seg, tiles)


def local(vectors, tiles, tile_rows, tile_cols, counts):
    nrow, ncol = lax.axis_size("row"), lax.axis_size("col")
    width, piece_len = vectors.shape
    per = piece_len // TILE

    def place(r, c):
        return (r % nrow) * ncol + c

    onward = [(place(r, (c + ncol // 2) % ncol), place(r + c, c)) for r in range(nrow) for c in range(ncol)]
    piece = vectors.reshape(width, per, TILE).transpose(1, 0, 2)
    copies, *data = stage(piece, tiles, tile_rows, tile_cols, counts, ncol)
    own = lax.all_to_all(copies, "col", split_axis=0, concat_axis=0, tiled=True)
    own_seg = own.reshape(ncol * per, width, TILE)
    other_seg = lax.ppermute(own_seg, AXES, onward)
    col_part = apply_tiles(True, own_seg, *data)
    home = lax.ppermute(col_part, AXES, [(b, a) for a, b in onward])
    row_part = apply_tiles(False, other_seg, *data)
    total = (row_part + home).reshape(ncol, per, width, TILE)
    pieces = lax.all_to_all(total, "col", split_axis=0, concat_axis=0, tiled=True)
    return pieces.sum(axis=0).transpose(1, 0, 2).reshape(width, piece_len)


def solution(mesh):
    placed = (
        P(None, AXES),
        P("row", "col", None, None),
        P("row", "col"),
        P("row", "col"),
        P("row", "col"),
    )
    return jax.shard_map(local, mesh=mesh, in_specs=placed, out_specs=P(None, AXES), check_vma=False)
```

time: 47.8 us -> 38.5 us (0.81)
  the two profiles are of different devices: /device:TPU:80 before, /device:TPU:65 now
where the time goes in v2:
time: 38.5 us; the launch traced here: 38.3 us
  blocking collectives  27.4 us (71%)
  Pallas kernels  4.8 us (12%)
  waiting for transfers between devices  3.08 us (8%)
  starting transfers between devices  1.72 us (4%)
  between operations  0.69 us (2%)
  other arithmetic  0.63 us (2%)
    all_to_all x1, blocking collectives, local(): lax.all_to_all(total, 'col', split_axis=0, concat_axis=0, tiled=True)  17.1 us
    all_to_all x1, blocking collectives, local(): own = lax.all_to_all(copies, 'col', split_axis=0, concat_axis=0, tiled=True)  10.3 us
    pallas_call x2, Pallas kernels, apply_tiles(): pl.pallas_call(functools.partial(tiles_kernel, mirrored), out_shape=jax.S...  2.64 us
    pallas_call x1, Pallas kernels, stage(): pl.pallas_call(stage_kernel, out_shape=[pltpu.VMEM((ncol, *vectors.shape)...  2.16 us
    ppermute x1, waiting for transfers between devices, local(): home = lax.ppermute(col_part, AXES, [(b, a) for a, b in onward])  1.92 us
    ppermute x1, starting transfers between devices, local(): other_seg = lax.ppermute(own_seg, AXES, onward)  1.63 us
    ppermute x1, waiting for transfers between devices, local(): other_seg = lax.ppermute(own_seg, AXES, onward)  1.16 us
  transfers between devices with their start and end apart: 2, of which 2 were waited for; matrix products, arithmetic and copies ran while one was open for 0% of the time, Pallas kernels for 7%

profile of v2, /device:TPU:65, one launch (start us, length us, event | category | flops | bytes accessed | tf_op | source)
XLA Modules:
  0.0 38.3 jit_solution(1483972063480982293)
XLA Ops:
  0.7 2.2 %shard_map.55 = (f32[8,4,8,128]{3,2,1,0:T(8,128)S(1)}, f32[1,48,128,128]{3,2,1,0:T(8,128)S(1)}, s32[1,48]{1,0:T(1,128)S(4)}, s32[1,48]{1,0:T(1,128)S(4)}, s32[1,1]{1,0:T(1,128)S(4)}) custom-call(f32[4,8,128]{2,1,0:T(8,128)} %bitcast.11, f32[1,48,128,128]{3,2,1,0:T(8,128)} %refs_1_.1, s32[1,48]{1,0:T(1,128)} %refs_2_.1, s32[1,48]{1,0:T(1,128)} %refs_3_.1, ...), custom_call_target="tpu_custom_call" | custom-call | bytes 3145728 | tf_op jit(solution)/shard_map/pallas_call | solution.py:38
  2.8 10.3 %all_to_all.10 = f32[8,4,8,128]{3,2,1,0:T(8,128)S(1)} all-to-all(f32[8,4,8,128]{3,2,1,0:T(8,128)S(1)} %get-tuple-element.13), channel_id=1, replica_groups=mesh['row'=32,'col'=8] {'col'}, dimensions={0} | all-to-all | bytes 262144 | tf_op jit(solution)/shard_map/all_to_all | solution.py:91
  13.1 1.6 %collective-permute-start = (f32[32,8,128]{2,1,0:T(8,128)S(1)}, f32[32,8,128]{2,1,0:T(8,128)S(1)}, u32[]{:S(2)}, u32[]{:S(2)}) collective-permute-start(f32[32,8,128]{2,1,0:T(8,128)S(1)} %bitcast.8), channel_id=1, source_target_pairs={{4,0},{5,9},{6,18},{7,27},{0,36},{1,45},{2,54},{3,63},{12,8},{13,1... | collective-permute-start | bytes 393224 | tf_op jit(solution)/shard_map/ppermute | solution.py:93
  14.7 0.9 %shard_map.57 = f32[32,8,128]{2,1,0:T(8,128)S(1)} custom-call(s32[1,1]{1,0:T(1,128)S(4)} %get-tuple-element.10.count_ref, s32[1,48]{1,0:T(1,128)S(4)} %get-tuple-element.11.rows_ref, s32[1,48]{1,0:T(1,128)S(4)} %get-tuple-element.12.cols_ref, f32[32,8,128]{2,1,0:T(8,128)S(1)} %bitcast.9, f32[1,48,128,128]{3,2,1,0:T(8,128)S(1)} %get-tuple-element.14.tiles_ref), custom_call_target="tpu_custom_call" | custom-call | flops 50331648 | bytes 3145728 | tf_op jit(solution)/shard_map/pallas_call | solution.py:68
  15.7 0.1 collective-permute-start.1
  15.8 1.2 %collective-permute-done.seg_ref = f32[32,8,128]{2,1,0:T(8,128)S(1)} collective-permute-done((f32[32,8,128]{2,1,0:T(8,128)S(1)}, f32[32,8,128]{2,1,0:T(8,128)S(1)}, u32[]{:S(2)}, u32[]{:S(2)}) %collective-permute-start) | collective-permute-done | bytes 131104 | tf_op jit(solution)/shard_map/ppermute | solution.py:93
  16.9 1.7 %shard_map.56 = f32[32,8,128]{2,1,0:T(8,128)S(1)} custom-call(s32[1,1]{1,0:T(1,128)S(4)} %get-tuple-element.10.count_ref, s32[1,48]{1,0:T(1,128)S(4)} %get-tuple-element.11.rows_ref, s32[1,48]{1,0:T(1,128)S(4)} %get-tuple-element.12.cols_ref, f32[32,8,128]{2,1,0:T(8,128)S(1)} %collective-permute-done.seg_ref, f32[1,48,128,128]{3,2,1,0:T(8,128)S(1)} %get-tuple-element.14.tiles_ref), custom_call_target="tpu_custom_call" | custom-call | flops 50331648 | bytes 3145728 | tf_op jit(solution)/shard_map/pallas_call | solution.py:68
  18.7 1.9 %collective-permute-done.1 = f32[32,8,128]{2,1,0:T(8,128)S(1)} collective-permute-done((f32[32,8,128]{2,1,0:T(8,128)S(1)}, f32[32,8,128]{2,1,0:T(8,128)S(1)}, u32[]{:S(2)}, u32[]{:S(2)}) %collective-permute-start.1) | collective-permute-done | bytes 131104 | tf_op jit(solution)/shard_map/ppermute | solution.py:95
  20.6 17.1 %all_to_all.11 = f32[8,4,8,128]{3,2,1,0:T(8,128)S(1)} all-to-all(f32[8,4,8,128]{3,2,1,0:T(8,128)S(1)} %bitcast.10), channel_id=1, replica_groups=mesh['row'=32,'col'=8] {'col'}, dimensions={0} | all-to-all | bytes 262144 | tf_op jit(solution)/shard_map/all_to_all | solution.py:98
  37.7 0.6 %reduce_sum.9 = f32[4,8,128]{2,1,0:T(8,128)} reduce(f32[8,4,8,128]{3,2,1,0:T(8,128)S(1)} %all_to_all.11, f32[]{:T(128)} %constant.0.clone.1), dimensions={0}, to_apply=%region_0.0 | reduce | flops 28672 | bytes 147460 | tf_op jit(solution)/shard_map/reduce_sum | solution.py:99
  (1 shorter events, 0.0 us)
Async XLA Ops:
  13.1 3.8 %collective-permute-start = (f32[32,8,128]{2,1,0:T(8,128)S(1)}, f32[32,8,128]{2,1,0:T(8,128)S(1)}, u32[]{:S(2)}, u32[]{:S(2)}) collective-permute-start(f32[32,8,128]{2,1,0:T(8,128)S(1)} %bitcast.8), channel_id=1, source_target_pairs={{4,0},{5,9},{6,18},{7,27},{0,36},{1,45},{2,54},{3,63},{12,8},{13,1... | collective-permute-start | bytes 393224 | tf_op jit(solution)/shard_map/ppermute | solution.py:93
  15.7 4.9 %collective-permute-start.1 = (f32[32,8,128]{2,1,0:T(8,128)S(1)}, f32[32,8,128]{2,1,0:T(8,128)S(1)}, u32[]{:S(2)}, u32[]{:S(2)}) collective-permute-start(f32[32,8,128]{2,1,0:T(8,128)S(1)} %shard_map.57), channel_id=1, source_target_pairs={{0,4},{9,5},{18,6},{27,7},{36,0},{45,1},{54,2},{63,3},{8,12},{17,1... | collective-permute-start | bytes 393224 | tf_op jit(solution)/shard_map/ppermute | solution.py:95

commit v3 on v2

v3 whole, which is shorter than its diff:
```python
import functools

import jax
import jax.numpy as jnp
from jax import lax
from jax.experimental import pallas as pl
from jax.experimental.pallas import tpu as pltpu
from jax.sharding import PartitionSpec as P

TILE = 128
CHUNKS = 4
AXES = ("row", "col")
SMEM = pl.BlockSpec(memory_space=pltpu.SMEM)
VMEM = pl.BlockSpec(memory_space=pltpu.VMEM)


def split(x):
    hi = x.astype(jnp.bfloat16)
    return hi, (x - hi.astype(jnp.float32)).astype(jnp.bfloat16)


def move_all(sources, targets, sems):
    moves = [pltpu.make_async_copy(s, t, sems.at[n]) for n, (s, t) in enumerate(zip(sources, targets, strict=True))]
    for move in moves:
        move.start()
    for move in moves:
        move.wait()


def stage_kernel(*refs):
    half = len(refs) // 2
    sources, targets = list(refs[:half]), list(refs[half:-1])
    chunk = sources[0].shape[1] // CHUNKS
    parts = [(0, pl.ds(n * chunk, chunk)) for n in range(CHUNKS)]
    move_all(
        [sources[0].at[p] for p in parts] + sources[1:], [targets[0].at[p] for p in parts] + targets[1:], refs[-1]
    )


HBM = pl.BlockSpec(memory_space=pltpu.HBM)


def stage(tiles, *scalars):
    return pl.pallas_call(
        stage_kernel,
        out_shape=[pltpu.VMEM(tiles.shape, tiles.dtype)] + [pltpu.SMEM(a.shape, a.dtype) for a in scalars],
        in_specs=[HBM] * (1 + len(scalars)),
        out_specs=[VMEM] + [SMEM] * len(scalars),
        scratch_shapes=[pltpu.SemaphoreType.DMA((CHUNKS + len(scalars),))],
        cost_estimate=pl.CostEstimate(flops=0, bytes_accessed=tiles.size * 4, transcendentals=0),
    )(tiles, *scalars)


def turn_kernel(tiles_ref, parts_ref):
    for t in range(tiles_ref.shape[1]):
        parts_ref[t, :, :TILE], parts_ref[t, :, TILE:] = split(tiles_ref[0, t].T)


def turn(tiles):
    slots = tiles.shape[1]
    parts = pltpu.VMEM((slots, TILE, 2 * TILE), jnp.bfloat16)
    return pl.pallas_call(
        turn_kernel,
        out_shape=[parts],
        in_specs=[VMEM],
        out_specs=[VMEM],
        compiler_params=pltpu.CompilerParams(vmem_limit_bytes=32 * 2**20),
        cost_estimate=pl.CostEstimate(flops=0, bytes_accessed=tiles.size * 8, transcendentals=0),
    )(tiles)


def products(slots, width, count_ref, from_ref, to_ref, seg_ref, parts_of, out_ref):
    out_ref[...] = jnp.zeros_like(out_ref)
    for t in range(slots):
        vec = jnp.where(t < count_ref[0, 0], seg_ref[from_ref[0, t]], 0.0)
        hi = vec.astype(jnp.bfloat16).astype(jnp.float32)
        both = jnp.concatenate([hi, vec - hi], axis=0).astype(jnp.bfloat16)
        got = jnp.dot(both, parts_of(t), preferred_element_type=jnp.float32)
        to = to_ref[0, t]
        out_ref[to] = out_ref[to] + (got[:width, :TILE] + (got[width:, :TILE] + got[:width, TILE:]))


def mirror_kernel(count_ref, rows_ref, cols_ref, seg_ref, tiles_ref, out_ref):
    slots, width = tiles_ref.shape[1], seg_ref.shape[1]
    products(slots, width, count_ref, rows_ref, cols_ref, seg_ref, lambda t: jnp.concatenate(split(tiles_ref[0, t]), axis=1), out_ref)


def plain_kernel(count_ref, rows_ref, cols_ref, seg_ref, parts_ref, out_ref):
    slots, width = parts_ref.shape[0], seg_ref.shape[1]
    products(slots, width, count_ref, cols_ref, rows_ref, seg_ref, lambda t: parts_ref[t], out_ref)


def apply_tiles(kernel, counts, tile_rows, tile_cols, seg, *tiles):
    slots = tile_rows.shape[1]
    return pl.pallas_call(
        kernel,
        out_shape=jax.ShapeDtypeStruct(seg.shape, jnp.float32),
        in_specs=[SMEM] * 3 + [VMEM] * (1 + len(tiles)),
        out_specs=VMEM,
        compiler_params=pltpu.CompilerParams(vmem_limit_bytes=32 * 2**20),
        cost_estimate=pl.CostEstimate(
            flops=2 * 4 * slots * 8 * TILE * TILE, bytes_accessed=slots * TILE * TILE * 4, transcendentals=0
        ),
    )(counts, tile_rows, tile_cols, seg, *tiles)


def local(vectors, tiles, tile_rows, tile_cols, counts):
    nrow, ncol = lax.axis_size("row"), lax.axis_size("col")
    width, piece_len = vectors.shape
    per = piece_len // TILE

    def place(r, c):
        return (r % nrow) * ncol + c

    half = ncol // 2

    def other(c):
        return (c + half) % ncol

    def sender(s, c):
        return other(c) if c % half == 0 or s % 2 == 0 else c

    onward = [(place(r, sender(r, c)), place(r + c, c)) for r in range(nrow) for c in range(ncol)]
    backward = [(place(r + c, c), place(r, other(c))) for r in range(nrow) for c in range(ncol)]
    piece = vectors.reshape(width, per, TILE).transpose(1, 0, 2)
    tiles, tile_rows, tile_cols = stage(tiles, tile_rows, tile_cols)
    places = (counts, tile_rows, tile_cols)
    own = lax.all_to_all(jnp.broadcast_to(piece[None], (ncol, *piece.shape)), "col", split_axis=0, concat_axis=0, tiled=True)
    own_seg = own.reshape(ncol * per, width, TILE)
    other_seg = lax.ppermute(own_seg, AXES, onward)
    col_part = apply_tiles(mirror_kernel, *places, own_seg, tiles)
    home = lax.ppermute(col_part, AXES, backward)
    row_part = apply_tiles(plain_kernel, *places, other_seg, *turn(tiles))
    total = (row_part + home).reshape(ncol, per, width, TILE)
    pieces = lax.all_to_all(total, "col", split_axis=0, concat_axis=0, tiled=True)
    return pieces.sum(axis=0).transpose(1, 0, 2).reshape(width, piece_len)


def solution(mesh):
    placed = (
        P(None, AXES),
        P("row", "col", None, None),
        P("row", "col"),
        P("row", "col"),
        P("row", "col"),
    )
    return jax.shard_map(local, mesh=mesh, in_specs=placed, out_specs=P(None, AXES), check_vma=False)
```

time: 38.5 us -> 36.5 us (0.948)
  the two profiles are of different devices: /device:TPU:65 before, /device:TPU:1 now
where the time goes in v3:
time: 36.5 us; the launch traced here: 36.2 us
  blocking collectives  15.8 us (43%)
  starting transfers between devices  7.58 us (21%)
  waiting for transfers between devices  6.28 us (17%)
  Pallas kernels  3.83 us (10%)
  local copies, waits for them, and re-layouts  1.37 us (4%)
  between operations  0.7 us (2%)
  other arithmetic  0.63 us (2%)
    all_to_all x1, blocking collectives, local(): lax.all_to_all(total, 'col', split_axis=0, concat_axis=0, tiled=True)  15.8 us
    all_to_all x1, starting transfers between devices, local(): lax.all_to_all(jnp.broadcast_to(piece[None], (ncol, *piece.shape)), 'col'...  5.86 us
    all_to_all x1, waiting for transfers between devices, local(): lax.all_to_all(jnp.broadcast_to(piece[None], (ncol, *piece.shape)), 'col'...  2.88 us
    ppermute x1, waiting for transfers between devices, local(): home = lax.ppermute(col_part, AXES, backward)  2.72 us
    pallas_call x1, Pallas kernels, stage(): pl.pallas_call(stage_kernel, out_shape=[pltpu.VMEM(tiles.shape, tiles.dty...  1.92 us
    ppermute x1, starting transfers between devices, local(): other_seg = lax.ppermute(own_seg, AXES, onward)  1.63 us
    broadcast_in_dim x1, local copies, waits for them, and re-layouts, local(): jnp.broadcast_to(piece[None], (ncol, *piece.shape))  1.37 us
    pallas_call x2, Pallas kernels, apply_tiles(): pl.pallas_call(kernel, out_shape=jax.ShapeDtypeStruct(seg.shape, jnp.floa...  1.04 us
  transfers between devices with their start and end apart: 3, of which 3 were waited for; matrix products, arithmetic and copies ran while one was open for 0% of the time, Pallas kernels for 11%

profile of v3, /device:TPU:1, one launch (start us, length us, event | category | flops | bytes accessed | tf_op | source)
XLA Modules:
  0.0 36.2 jit_solution(17871972407623549816)
XLA Ops:
  0.0 1.4 %broadcast_in_dim.2 = f32[8,4,8,128]{3,2,1,0:T(8,128)} broadcast(f32[4,8,128]{2,1,0:T(8,128)} %bitcast.11), dimensions={1,2,3} | broadcast | bytes 147456 | tf_op jit(solution)/shard_map/broadcast_in_dim | solution.py:128
  1.4 5.9 %all-to-all-start = ((f32[8,4,8,128]{3,2,1,0:T(8,128)}), f32[8,4,8,128]{3,2,1,0:T(8,128)S(1)}, u32[]{:S(2)}, u32[]{:S(2)}) async-start(f32[8,4,8,128]{3,2,1,0:T(8,128)} %broadcast_in_dim.2), calls=%async_computation | async-start | bytes 262144 | tf_op jit(solution)/shard_map/all_to_all | solution.py:128
  7.9 1.9 %shard_map.55 = (f32[1,48,128,128]{3,2,1,0:T(8,128)S(1)}, s32[1,48]{1,0:T(1,128)S(4)}, s32[1,48]{1,0:T(1,128)S(4)}) custom-call(f32[1,48,128,128]{3,2,1,0:T(8,128)} %refs_0_.1, s32[1,48]{1,0:T(1,128)} %refs_1_.1, s32[1,48]{1,0:T(1,128)} %refs_2_.1), custom_call_target="tpu_custom_call" | custom-call | bytes 3145728 | tf_op jit(solution)/shard_map/pallas_call | solution.py:44
  9.8 2.9 %all-to-all-done = f32[8,4,8,128]{3,2,1,0:T(8,128)S(1)} async-done(((f32[8,4,8,128]{3,2,1,0:T(8,128)}), f32[8,4,8,128]{3,2,1,0:T(8,128)S(1)}, u32[]{:S(2)}, u32[]{:S(2)}) %all-to-all-start) | async-done | bytes 131104 | tf_op jit(solution)/shard_map/all_to_all | solution.py:128
  12.7 1.6 %collective-permute-start = (f32[32,8,128]{2,1,0:T(8,128)S(1)}, f32[32,8,128]{2,1,0:T(8,128)S(1)}, u32[]{:S(2)}, u32[]{:S(2)}) collective-permute-start(f32[32,8,128]{2,1,0:T(8,128)S(1)} %bitcast.8), channel_id=1, source_target_pairs={{4,0},{5,9},{6,18},{7,27},{0,36},{1,45},{2,54},{3,63},{12,8},{9,17... | collective-permute-start | bytes 393224 | tf_op jit(solution)/shard_map/ppermute | solution.py:130
  14.3 0.5 %shard_map.58 = f32[32,8,128]{2,1,0:T(8,128)S(1)} custom-call(s32[1,1]{1,0:T(1,128)S(6)} %copy.6.count_ref, s32[1,48]{1,0:T(1,128)S(4)} %get-tuple-element.8.rows_ref, s32[1,48]{1,0:T(1,128)S(4)} %get-tuple-element.9.cols_ref, f32[32,8,128]{2,1,0:T(8,128)S(1)} %bitcast.9, f32[1,48,128,128]{3,2,1,0:T(8,128)S(1)} %get-tuple-element.10.tiles_ref), custom_call_target="tpu_custom_call" | custom-call | flops 50331648 | bytes 3145728 | tf_op jit(solution)/shard_map/pallas_call | solution.py:95
  14.9 0.1 collective-permute-start.1
  14.9 0.9 %shard_map.56.parts_ref = bf16[48,128,256]{2,1,0:T(8,128)(2,1)S(1)} custom-call(f32[1,48,128,128]{3,2,1,0:T(8,128)S(1)} %get-tuple-element.10.tiles_ref), custom_call_target="tpu_custom_call" | custom-call | bytes 6291456 | tf_op jit(solution)/shard_map/pallas_call | solution.py:62
  15.8 0.7 %collective-permute-done.seg_ref = f32[32,8,128]{2,1,0:T(8,128)S(1)} collective-permute-done((f32[32,8,128]{2,1,0:T(8,128)S(1)}, f32[32,8,128]{2,1,0:T(8,128)S(1)}, u32[]{:S(2)}, u32[]{:S(2)}) %collective-permute-start) | collective-permute-done | bytes 131104 | tf_op jit(solution)/shard_map/ppermute | solution.py:130
  16.5 0.5 %shard_map.57 = f32[32,8,128]{2,1,0:T(8,128)S(1)} custom-call(s32[1,1]{1,0:T(1,128)S(6)} %copy.6.count_ref, s32[1,48]{1,0:T(1,128)S(4)} %get-tuple-element.8.rows_ref, s32[1,48]{1,0:T(1,128)S(4)} %get-tuple-element.9.cols_ref, f32[32,8,128]{2,1,0:T(8,128)S(1)} %collective-permute-done.seg_ref, bf16[48,128,256]{2,1,0:T(8,128)(2,1)S(1)} %shard_map.56.parts_ref), custom_call_target="tpu_custom_call" | custom-call | flops 50331648 | bytes 3145728 | tf_op jit(solution)/shard_map/pallas_call | solution.py:95
  17.0 2.7 %collective-permute-done.1 = f32[32,8,128]{2,1,0:T(8,128)S(1)} collective-permute-done((f32[32,8,128]{2,1,0:T(8,128)S(1)}, f32[32,8,128]{2,1,0:T(8,128)S(1)}, u32[]{:S(2)}, u32[]{:S(2)}) %collective-permute-start.1) | collective-permute-done | bytes 131104 | tf_op jit(solution)/shard_map/ppermute | solution.py:132
  19.8 15.8 %all_to_all.10 = f32[8,4,8,128]{3,2,1,0:T(8,128)S(1)} all-to-all(f32[8,4,8,128]{3,2,1,0:T(8,128)S(1)} %bitcast.10), channel_id=1, replica_groups=mesh['row'=32,'col'=8] {'col'}, dimensions={0} | all-to-all | bytes 262144 | tf_op jit(solution)/shard_map/all_to_all | solution.py:135
  35.6 0.6 %reduce_sum.9 = f32[4,8,128]{2,1,0:T(8,128)} reduce(f32[8,4,8,128]{3,2,1,0:T(8,128)S(1)} %all_to_all.10, f32[]{:T(128)} %constant.0.clone.1), dimensions={0}, to_apply=%region_0.0 | reduce | flops 28672 | bytes 147460 | tf_op jit(solution)/shard_map/reduce_sum | solution.py:136
  (1 shorter events, 0.0 us)
Async XLA Ops:
  1.4 11.3 %all-to-all-start = ((f32[8,4,8,128]{3,2,1,0:T(8,128)}), f32[8,4,8,128]{3,2,1,0:T(8,128)S(1)}, u32[]{:S(2)}, u32[]{:S(2)}) async-start(f32[8,4,8,128]{3,2,1,0:T(8,128)} %broadcast_in_dim.2), calls=%async_computation | async-start | bytes 262144 | tf_op jit(solution)/shard_map/all_to_all | solution.py:128
  12.7 3.8 %collective-permute-start = (f32[32,8,128]{2,1,0:T(8,128)S(1)}, f32[32,8,128]{2,1,0:T(8,128)S(1)}, u32[]{:S(2)}, u32[]{:S(2)}) collective-permute-start(f32[32,8,128]{2,1,0:T(8,128)S(1)} %bitcast.8), channel_id=1, source_target_pairs={{4,0},{5,9},{6,18},{7,27},{0,36},{1,45},{2,54},{3,63},{12,8},{9,17... | collective-permute-start | bytes 393224 | tf_op jit(solution)/shard_map/ppermute | solution.py:130
  14.9 4.9 %collective-permute-start.1 = (f32[32,8,128]{2,1,0:T(8,128)S(1)}, f32[32,8,128]{2,1,0:T(8,128)S(1)}, u32[]{:S(2)}, u32[]{:S(2)}) collective-permute-start(f32[32,8,128]{2,1,0:T(8,128)S(1)} %shard_map.58), channel_id=1, source_target_pairs={{0,4},{9,5},{18,6},{27,7},{36,0},{45,1},{54,2},{63,3},{8,12},{17,1... | collective-permute-start | bytes 393224 | tf_op jit(solution)/shard_map/ppermute | solution.py:132

commit v4 on v3

--- a/solution.py
+++ b/solution.py
@@ -9,6 +9,7 @@
 
 TILE = 128
 CHUNKS = 4
+SWAPS = (10, 0, 10, 8)
 AXES = ("row", "col")
 SMEM = pl.BlockSpec(memory_space=pltpu.SMEM)
 VMEM = pl.BlockSpec(memory_space=pltpu.VMEM)
@@ -118,7 +119,7 @@
         return (c + half) % ncol
 
     def sender(s, c):
-        return other(c) if c % half == 0 or s % 2 == 0 else c
+        return other(c) if c % half == 0 or SWAPS[s % 4] >> c % half & 1 else c
 
     onward = [(place(r, sender(r, c)), place(r + c, c)) for r in range(nrow) for c in range(ncol)]
     backward = [(place(r + c, c), place(r, other(c))) for r in range(nrow) for c in range(ncol)]

time: 36.5 us -> 36.5 us (level)
  no operation moved by 1% of the time
where the time goes in v4:
time: 36.5 us; the launch traced here: 35.9 us
  blocking collectives  15.5 us (42%)
  starting transfers between devices  7.58 us (21%)
  waiting for transfers between devices  6.28 us (17%)
  Pallas kernels  3.83 us (10%)
  local copies, waits for them, and re-layouts  1.37 us (4%)
  between operations  0.7 us (2%)
  other arithmetic  0.63 us (2%)
    all_to_all x1, blocking collectives, local(): lax.all_to_all(total, 'col', split_axis=0, concat_axis=0, tiled=True)  15.5 us
    all_to_all x1, starting transfers between devices, local(): lax.all_to_all(jnp.broadcast_to(piece[None], (ncol, *piece.shape)), 'col'...  5.86 us
    all_to_all x1, waiting for transfers between devices, local(): lax.all_to_all(jnp.broadcast_to(piece[None], (ncol, *piece.shape)), 'col'...  2.88 us
    ppermute x1, waiting for transfers between devices, local(): home = lax.ppermute(col_part, AXES, backward)  2.73 us
    pallas_call x1, Pallas kernels, stage(): pl.pallas_call(stage_kernel, out_shape=[pltpu.VMEM(tiles.shape, tiles.dty...  1.92 us
    ppermute x1, starting transfers between devices, local(): other_seg = lax.ppermute(own_seg, AXES, onward)  1.63 us
    broadcast_in_dim x1, local copies, waits for them, and re-layouts, local(): jnp.broadcast_to(piece[None], (ncol, *piece.shape))  1.37 us
    pallas_call x2, Pallas kernels, apply_tiles(): pl.pallas_call(kernel, out_shape=jax.ShapeDtypeStruct(seg.shape, jnp.floa...  1.04 us
  transfers between devices with their start and end apart: 3, of which 3 were waited for; matrix products, arithmetic and copies ran while one was open for 0% of the time, Pallas kernels for 11%

profile of v4, /device:TPU:1, one launch (start us, length us, event | category | flops | bytes accessed | tf_op | source)
XLA Modules:
  0.0 35.9 jit_solution(5324916595123537738)
XLA Ops:
  0.0 1.4 %broadcast_in_dim.2 = f32[8,4,8,128]{3,2,1,0:T(8,128)} broadcast(f32[4,8,128]{2,1,0:T(8,128)} %bitcast.11), dimensions={1,2,3} | broadcast | bytes 147456 | tf_op jit(solution)/shard_map/broadcast_in_dim | solution.py:129
  1.4 5.9 %all-to-all-start = ((f32[8,4,8,128]{3,2,1,0:T(8,128)}), f32[8,4,8,128]{3,2,1,0:T(8,128)S(1)}, u32[]{:S(2)}, u32[]{:S(2)}) async-start(f32[8,4,8,128]{3,2,1,0:T(8,128)} %broadcast_in_dim.2), calls=%async_computation | async-start | bytes 262144 | tf_op jit(solution)/shard_map/all_to_all | solution.py:129
  7.9 1.9 %shard_map.55 = (f32[1,48,128,128]{3,2,1,0:T(8,128)S(1)}, s32[1,48]{1,0:T(1,128)S(4)}, s32[1,48]{1,0:T(1,128)S(4)}) custom-call(f32[1,48,128,128]{3,2,1,0:T(8,128)} %refs_0_.1, s32[1,48]{1,0:T(1,128)} %refs_1_.1, s32[1,48]{1,0:T(1,128)} %refs_2_.1), custom_call_target="tpu_custom_call" | custom-call | bytes 3145728 | tf_op jit(solution)/shard_map/pallas_call | solution.py:45
  9.8 2.9 %all-to-all-done = f32[8,4,8,128]{3,2,1,0:T(8,128)S(1)} async-done(((f32[8,4,8,128]{3,2,1,0:T(8,128)}), f32[8,4,8,128]{3,2,1,0:T(8,128)S(1)}, u32[]{:S(2)}, u32[]{:S(2)}) %all-to-all-start) | async-done | bytes 131104 | tf_op jit(solution)/shard_map/all_to_all | solution.py:129
  12.7 1.6 %collective-permute-start = (f32[32,8,128]{2,1,0:T(8,128)S(1)}, f32[32,8,128]{2,1,0:T(8,128)S(1)}, u32[]{:S(2)}, u32[]{:S(2)}) collective-permute-start(f32[32,8,128]{2,1,0:T(8,128)S(1)} %bitcast.8), channel_id=1, source_target_pairs={{4,0},{5,9},{2,18},{7,27},{0,36},{1,45},{6,54},{3,63},{12,8},{9,17... | collective-permute-start | bytes 393224 | tf_op jit(solution)/shard_map/ppermute | solution.py:131
  14.3 0.5 %shard_map.58 = f32[32,8,128]{2,1,0:T(8,128)S(1)} custom-call(s32[1,1]{1,0:T(1,128)S(6)} %copy.6.count_ref, s32[1,48]{1,0:T(1,128)S(4)} %get-tuple-element.8.rows_ref, s32[1,48]{1,0:T(1,128)S(4)} %get-tuple-element.9.cols_ref, f32[32,8,128]{2,1,0:T(8,128)S(1)} %bitcast.9, f32[1,48,128,128]{3,2,1,0:T(8,128)S(1)} %get-tuple-element.10.tiles_ref), custom_call_target="tpu_custom_call" | custom-call | flops 50331648 | bytes 3145728 | tf_op jit(solution)/shard_map/pallas_call | solution.py:96
  14.9 0.1 collective-permute-start.1
  15.0 0.9 %shard_map.56.parts_ref = bf16[48,128,256]{2,1,0:T(8,128)(2,1)S(1)} custom-call(f32[1,48,128,128]{3,2,1,0:T(8,128)S(1)} %get-tuple-element.10.tiles_ref), custom_call_target="tpu_custom_call" | custom-call | bytes 6291456 | tf_op jit(solution)/shard_map/pallas_call | solution.py:63
  15.8 0.7 %collective-permute-done.seg_ref = f32[32,8,128]{2,1,0:T(8,128)S(1)} collective-permute-done((f32[32,8,128]{2,1,0:T(8,128)S(1)}, f32[32,8,128]{2,1,0:T(8,128)S(1)}, u32[]{:S(2)}, u32[]{:S(2)}) %collective-permute-start) | collective-permute-done | bytes 131104 | tf_op jit(solution)/shard_map/ppermute | solution.py:131
  16.5 0.5 %shard_map.57 = f32[32,8,128]{2,1,0:T(8,128)S(1)} custom-call(s32[1,1]{1,0:T(1,128)S(6)} %copy.6.count_ref, s32[1,48]{1,0:T(1,128)S(4)} %get-tuple-element.8.rows_ref, s32[1,48]{1,0:T(1,128)S(4)} %get-tuple-element.9.cols_ref, f32[32,8,128]{2,1,0:T(8,128)S(1)} %collective-permute-done.seg_ref, bf16[48,128,256]{2,1,0:T(8,128)(2,1)S(1)} %shard_map.56.parts_ref), custom_call_target="tpu_custom_call" | custom-call | flops 50331648 | bytes 3145728 | tf_op jit(solution)/shard_map/pallas_call | solution.py:96
  17.0 2.7 %collective-permute-done.1 = f32[32,8,128]{2,1,0:T(8,128)S(1)} collective-permute-done((f32[32,8,128]{2,1,0:T(8,128)S(1)}, f32[32,8,128]{2,1,0:T(8,128)S(1)}, u32[]{:S(2)}, u32[]{:S(2)}) %collective-permute-start.1) | collective-permute-done | bytes 131104 | tf_op jit(solution)/shard_map/ppermute | solution.py:133
  19.8 15.5 %all_to_all.10 = f32[8,4,8,128]{3,2,1,0:T(8,128)S(1)} all-to-all(f32[8,4,8,128]{3,2,1,0:T(8,128)S(1)} %bitcast.10), channel_id=1, replica_groups=mesh['row'=32,'col'=8] {'col'}, dimensions={0} | all-to-all | bytes 262144 | tf_op jit(solution)/shard_map/all_to_all | solution.py:136
  35.3 0.6 %reduce_sum.9 = f32[4,8,128]{2,1,0:T(8,128)} reduce(f32[8,4,8,128]{3,2,1,0:T(8,128)S(1)} %all_to_all.10, f32[]{:T(128)} %constant.0.clone.1), dimensions={0}, to_apply=%region_0.0 | reduce | flops 28672 | bytes 147460 | tf_op jit(solution)/shard_map/reduce_sum | solution.py:137
  (1 shorter events, 0.0 us)
Async XLA Ops:
  1.4 11.3 %all-to-all-start = ((f32[8,4,8,128]{3,2,1,0:T(8,128)}), f32[8,4,8,128]{3,2,1,0:T(8,128)S(1)}, u32[]{:S(2)}, u32[]{:S(2)}) async-start(f32[8,4,8,128]{3,2,1,0:T(8,128)} %broadcast_in_dim.2), calls=%async_computation | async-start | bytes 262144 | tf_op jit(solution)/shard_map/all_to_all | solution.py:129
  12.7 3.8 %collective-permute-start = (f32[32,8,128]{2,1,0:T(8,128)S(1)}, f32[32,8,128]{2,1,0:T(8,128)S(1)}, u32[]{:S(2)}, u32[]{:S(2)}) collective-permute-start(f32[32,8,128]{2,1,0:T(8,128)S(1)} %bitcast.8), channel_id=1, source_target_pairs={{4,0},{5,9},{2,18},{7,27},{0,36},{1,45},{6,54},{3,63},{12,8},{9,17... | collective-permute-start | bytes 393224 | tf_op jit(solution)/shard_map/ppermute | solution.py:131
  14.9 4.9 %collective-permute-start.1 = (f32[32,8,128]{2,1,0:T(8,128)S(1)}, f32[32,8,128]{2,1,0:T(8,128)S(1)}, u32[]{:S(2)}, u32[]{:S(2)}) collective-permute-start(f32[32,8,128]{2,1,0:T(8,128)S(1)} %shard_map.58), channel_id=1, source_target_pairs={{0,4},{9,5},{18,6},{27,7},{36,0},{45,1},{54,2},{63,3},{8,12},{17,1... | collective-permute-start | bytes 393224 | tf_op jit(solution)/shard_map/ppermute | solution.py:133

commit v5 on v4

--- a/solution.py
+++ b/solution.py
@@ -9,7 +9,7 @@
 
 TILE = 128
 CHUNKS = 4
-SWAPS = (10, 0, 10, 8)
+SWAPS = (10, 0, 2, 8)
 AXES = ("row", "col")
 SMEM = pl.BlockSpec(memory_space=pltpu.SMEM)
 VMEM = pl.BlockSpec(memory_space=pltpu.VMEM)

time: 36.5 us -> 36.3 us (level)
  no operation moved by 1% of the time
where the time goes in v5:
time: 36.3 us; the launch traced here: 35.9 us
  blocking collectives  15.5 us (43%)
  starting transfers between devices  7.58 us (21%)
  waiting for transfers between devices  6.28 us (17%)
  Pallas kernels  3.83 us (11%)
  local copies, waits for them, and re-layouts  1.37 us (4%)
  between operations  0.7 us (2%)
  other arithmetic  0.63 us (2%)
    all_to_all x1, blocking collectives, local(): lax.all_to_all(total, 'col', split_axis=0, concat_axis=0, tiled=True)  15.5 us
    all_to_all x1, starting transfers between devices, local(): lax.all_to_all(jnp.broadcast_to(piece[None], (ncol, *piece.shape)), 'col'...  5.86 us
    all_to_all x1, waiting for transfers between devices, local(): lax.all_to_all(jnp.broadcast_to(piece[None], (ncol, *piece.shape)), 'col'...  2.88 us
    ppermute x1, waiting for transfers between devices, local(): home = lax.ppermute(col_part, AXES, backward)  2.72 us
    pallas_call x1, Pallas kernels, stage(): pl.pallas_call(stage_kernel, out_shape=[pltpu.VMEM(tiles.shape, tiles.dty...  1.92 us
    ppermute x1, starting transfers between devices, local(): other_seg = lax.ppermute(own_seg, AXES, onward)  1.63 us
    broadcast_in_dim x1, local copies, waits for them, and re-layouts, local(): jnp.broadcast_to(piece[None], (ncol, *piece.shape))  1.37 us
    pallas_call x2, Pallas kernels, apply_tiles(): pl.pallas_call(kernel, out_shape=jax.ShapeDtypeStruct(seg.shape, jnp.floa...  1.04 us
  transfers between devices with their start and end apart: 3, of which 3 were waited for; matrix products, arithmetic and copies ran while one was open for 0% of the time, Pallas kernels for 11%

profile of v5, /device:TPU:1, one launch (start us, length us, event | category | flops | bytes accessed | tf_op | source)
XLA Modules:
  0.0 35.9 jit_solution(5466786784442993810)
XLA Ops:
  0.0 1.4 %broadcast_in_dim.2 = f32[8,4,8,128]{3,2,1,0:T(8,128)} broadcast(f32[4,8,128]{2,1,0:T(8,128)} %bitcast.11), dimensions={1,2,3} | broadcast | bytes 147456 | tf_op jit(solution)/shard_map/broadcast_in_dim | solution.py:129
  1.4 5.9 %all-to-all-start = ((f32[8,4,8,128]{3,2,1,0:T(8,128)}), f32[8,4,8,128]{3,2,1,0:T(8,128)S(1)}, u32[]{:S(2)}, u32[]{:S(2)}) async-start(f32[8,4,8,128]{3,2,1,0:T(8,128)} %broadcast_in_dim.2), calls=%async_computation | async-start | bytes 262144 | tf_op jit(solution)/shard_map/all_to_all | solution.py:129
  7.9 1.9 %shard_map.55 = (f32[1,48,128,128]{3,2,1,0:T(8,128)S(1)}, s32[1,48]{1,0:T(1,128)S(4)}, s32[1,48]{1,0:T(1,128)S(4)}) custom-call(f32[1,48,128,128]{3,2,1,0:T(8,128)} %refs_0_.1, s32[1,48]{1,0:T(1,128)} %refs_1_.1, s32[1,48]{1,0:T(1,128)} %refs_2_.1), custom_call_target="tpu_custom_call" | custom-call | bytes 3145728 | tf_op jit(solution)/shard_map/pallas_call | solution.py:45
  9.8 2.9 %all-to-all-done = f32[8,4,8,128]{3,2,1,0:T(8,128)S(1)} async-done(((f32[8,4,8,128]{3,2,1,0:T(8,128)}), f32[8,4,8,128]{3,2,1,0:T(8,128)S(1)}, u32[]{:S(2)}, u32[]{:S(2)}) %all-to-all-start) | async-done | bytes 131104 | tf_op jit(solution)/shard_map/all_to_all | solution.py:129
  12.7 1.6 %collective-permute-start = (f32[32,8,128]{2,1,0:T(8,128)S(1)}, f32[32,8,128]{2,1,0:T(8,128)S(1)}, u32[]{:S(2)}, u32[]{:S(2)}) collective-permute-start(f32[32,8,128]{2,1,0:T(8,128)S(1)} %bitcast.8), channel_id=1, source_target_pairs={{4,0},{5,9},{2,18},{7,27},{0,36},{1,45},{6,54},{3,63},{12,8},{9,17... | collective-permute-start | bytes 393224 | tf_op jit(solution)/shard_map/ppermute | solution.py:131
  14.3 0.5 %shard_map.58 = f32[32,8,128]{2,1,0:T(8,128)S(1)} custom-call(s32[1,1]{1,0:T(1,128)S(6)} %copy.6.count_ref, s32[1,48]{1,0:T(1,128)S(4)} %get-tuple-element.8.rows_ref, s32[1,48]{1,0:T(1,128)S(4)} %get-tuple-element.9.cols_ref, f32[32,8,128]{2,1,0:T(8,128)S(1)} %bitcast.9, f32[1,48,128,128]{3,2,1,0:T(8,128)S(1)} %get-tuple-element.10.tiles_ref), custom_call_target="tpu_custom_call" | custom-call | flops 50331648 | bytes 3145728 | tf_op jit(solution)/shard_map/pallas_call | solution.py:96
  14.9 0.1 collective-permute-start.1
  14.9 0.9 %shard_map.56.parts_ref = bf16[48,128,256]{2,1,0:T(8,128)(2,1)S(1)} custom-call(f32[1,48,128,128]{3,2,1,0:T(8,128)S(1)} %get-tuple-element.10.tiles_ref), custom_call_target="tpu_custom_call" | custom-call | bytes 6291456 | tf_op jit(solution)/shard_map/pallas_call | solution.py:63
  15.8 0.7 %collective-permute-done.seg_ref = f32[32,8,128]{2,1,0:T(8,128)S(1)} collective-permute-done((f32[32,8,128]{2,1,0:T(8,128)S(1)}, f32[32,8,128]{2,1,0:T(8,128)S(1)}, u32[]{:S(2)}, u32[]{:S(2)}) %collective-permute-start) | collective-permute-done | bytes 131104 | tf_op jit(solution)/shard_map/ppermute | solution.py:131
  16.5 0.5 %shard_map.57 = f32[32,8,128]{2,1,0:T(8,128)S(1)} custom-call(s32[1,1]{1,0:T(1,128)S(6)} %copy.6.count_ref, s32[1,48]{1,0:T(1,128)S(4)} %get-tuple-element.8.rows_ref, s32[1,48]{1,0:T(1,128)S(4)} %get-tuple-element.9.cols_ref, f32[32,8,128]{2,1,0:T(8,128)S(1)} %collective-permute-done.seg_ref, bf16[48,128,256]{2,1,0:T(8,128)(2,1)S(1)} %shard_map.56.parts_ref), custom_call_target="tpu_custom_call" | custom-call | flops 50331648 | bytes 3145728 | tf_op jit(solution)/shard_map/pallas_call | solution.py:96
  17.0 2.7 %collective-permute-done.1 = f32[32,8,128]{2,1,0:T(8,128)S(1)} collective-permute-done((f32[32,8,128]{2,1,0:T(8,128)S(1)}, f32[32,8,128]{2,1,0:T(8,128)S(1)}, u32[]{:S(2)}, u32[]{:S(2)}) %collective-permute-start.1) | collective-permute-done | bytes 131104 | tf_op jit(solution)/shard_map/ppermute | solution.py:133
  19.8 15.5 %all_to_all.10 = f32[8,4,8,128]{3,2,1,0:T(8,128)S(1)} all-to-all(f32[8,4,8,128]{3,2,1,0:T(8,128)S(1)} %bitcast.10), channel_id=1, replica_groups=mesh['row'=32,'col'=8] {'col'}, dimensions={0} | all-to-all | bytes 262144 | tf_op jit(solution)/shard_map/all_to_all | solution.py:136
  35.3 0.6 %reduce_sum.9 = f32[4,8,128]{2,1,0:T(8,128)} reduce(f32[8,4,8,128]{3,2,1,0:T(8,128)S(1)} %all_to_all.10, f32[]{:T(128)} %constant.0.clone.1), dimensions={0}, to_apply=%region_0.0 | reduce | flops 28672 | bytes 147460 | tf_op jit(solution)/shard_map/reduce_sum | solution.py:137
  (1 shorter events, 0.0 us)
Async XLA Ops:
  1.4 11.3 %all-to-all-start = ((f32[8,4,8,128]{3,2,1,0:T(8,128)}), f32[8,4,8,128]{3,2,1,0:T(8,128)S(1)}, u32[]{:S(2)}, u32[]{:S(2)}) async-start(f32[8,4,8,128]{3,2,1,0:T(8,128)} %broadcast_in_dim.2), calls=%async_computation | async-start | bytes 262144 | tf_op jit(solution)/shard_map/all_to_all | solution.py:129
  12.7 3.8 %collective-permute-start = (f32[32,8,128]{2,1,0:T(8,128)S(1)}, f32[32,8,128]{2,1,0:T(8,128)S(1)}, u32[]{:S(2)}, u32[]{:S(2)}) collective-permute-start(f32[32,8,128]{2,1,0:T(8,128)S(1)} %bitcast.8), channel_id=1, source_target_pairs={{4,0},{5,9},{2,18},{7,27},{0,36},{1,45},{6,54},{3,63},{12,8},{9,17... | collective-permute-start | bytes 393224 | tf_op jit(solution)/shard_map/ppermute | solution.py:131
  14.9 4.9 %collective-permute-start.1 = (f32[32,8,128]{2,1,0:T(8,128)S(1)}, f32[32,8,128]{2,1,0:T(8,128)S(1)}, u32[]{:S(2)}, u32[]{:S(2)}) collective-permute-start(f32[32,8,128]{2,1,0:T(8,128)S(1)} %shard_map.58), channel_id=1, source_target_pairs={{0,4},{9,5},{18,6},{27,7},{36,0},{45,1},{54,2},{63,3},{8,12},{17,1... | collective-permute-start | bytes 393224 | tf_op jit(solution)/shard_map/ppermute | solution.py:133

commit v6 on v5

--- a/solution.py
+++ b/solution.py
@@ -9,7 +9,7 @@
 
 TILE = 128
 CHUNKS = 4
-SWAPS = (10, 0, 2, 8)
+SWAPS = (10, 2, 2, 10)
 AXES = ("row", "col")
 SMEM = pl.BlockSpec(memory_space=pltpu.SMEM)
 VMEM = pl.BlockSpec(memory_space=pltpu.VMEM)

time: 36.3 us -> 36.3 us (level)
  no operation moved by 1% of the time
where the time goes in v6:
time: 36.3 us; the launch traced here: 35.9 us
  blocking collectives  15.5 us (43%)
  starting transfers between devices  7.58 us (21%)
  waiting for transfers between devices  6.28 us (17%)
  Pallas kernels  3.83 us (11%)
  local copies, waits for them, and re-layouts  1.37 us (4%)
  between operations  0.7 us (2%)
  other arithmetic  0.63 us (2%)
    all_to_all x1, blocking collectives, local(): lax.all_to_all(total, 'col', split_axis=0, concat_axis=0, tiled=True)  15.5 us
    all_to_all x1, starting transfers between devices, local(): lax.all_to_all(jnp.broadcast_to(piece[None], (ncol, *piece.shape)), 'col'...  5.86 us
    all_to_all x1, waiting for transfers between devices, local(): lax.all_to_all(jnp.broadcast_to(piece[None], (ncol, *piece.shape)), 'col'...  2.88 us
    ppermute x1, waiting for transfers between devices, local(): home = lax.ppermute(col_part, AXES, backward)  2.72 us
    pallas_call x1, Pallas kernels, stage(): pl.pallas_call(stage_kernel, out_shape=[pltpu.VMEM(tiles.shape, tiles.dty...  1.92 us
    ppermute x1, starting transfers between devices, local(): other_seg = lax.ppermute(own_seg, AXES, onward)  1.63 us
    broadcast_in_dim x1, local copies, waits for them, and re-layouts, local(): jnp.broadcast_to(piece[None], (ncol, *piece.shape))  1.37 us
    pallas_call x2, Pallas kernels, apply_tiles(): pl.pallas_call(kernel, out_shape=jax.ShapeDtypeStruct(seg.shape, jnp.floa...  1.04 us
  transfers between devices with their start and end apart: 3, of which 3 were waited for; matrix products, arithmetic and copies ran while one was open for 0% of the time, Pallas kernels for 11%

profile of v6, /device:TPU:1, one launch (start us, length us, event | category | flops | bytes accessed | tf_op | source)
XLA Modules:
  0.0 35.9 jit_solution(8912377478654197994)
XLA Ops:
  0.0 1.4 %broadcast_in_dim.2 = f32[8,4,8,128]{3,2,1,0:T(8,128)} broadcast(f32[4,8,128]{2,1,0:T(8,128)} %bitcast.11), dimensions={1,2,3} | broadcast | bytes 147456 | tf_op jit(solution)/shard_map/broadcast_in_dim | solution.py:129
  1.4 5.9 %all-to-all-start = ((f32[8,4,8,128]{3,2,1,0:T(8,128)}), f32[8,4,8,128]{3,2,1,0:T(8,128)S(1)}, u32[]{:S(2)}, u32[]{:S(2)}) async-start(f32[8,4,8,128]{3,2,1,0:T(8,128)} %broadcast_in_dim.2), calls=%async_computation | async-start | bytes 262144 | tf_op jit(solution)/shard_map/all_to_all | solution.py:129
  7.9 1.9 %shard_map.55 = (f32[1,48,128,128]{3,2,1,0:T(8,128)S(1)}, s32[1,48]{1,0:T(1,128)S(4)}, s32[1,48]{1,0:T(1,128)S(4)}) custom-call(f32[1,48,128,128]{3,2,1,0:T(8,128)} %refs_0_.1, s32[1,48]{1,0:T(1,128)} %refs_1_.1, s32[1,48]{1,0:T(1,128)} %refs_2_.1), custom_call_target="tpu_custom_call" | custom-call | bytes 3145728 | tf_op jit(solution)/shard_map/pallas_call | solution.py:45
  9.8 2.9 %all-to-all-done = f32[8,4,8,128]{3,2,1,0:T(8,128)S(1)} async-done(((f32[8,4,8,128]{3,2,1,0:T(8,128)}), f32[8,4,8,128]{3,2,1,0:T(8,128)S(1)}, u32[]{:S(2)}, u32[]{:S(2)}) %all-to-all-start) | async-done | bytes 131104 | tf_op jit(solution)/shard_map/all_to_all | solution.py:129
  12.7 1.6 %collective-permute-start = (f32[32,8,128]{2,1,0:T(8,128)S(1)}, f32[32,8,128]{2,1,0:T(8,128)S(1)}, u32[]{:S(2)}, u32[]{:S(2)}) collective-permute-start(f32[32,8,128]{2,1,0:T(8,128)S(1)} %bitcast.8), channel_id=1, source_target_pairs={{4,0},{5,9},{2,18},{7,27},{0,36},{1,45},{6,54},{3,63},{12,8},{13,1... | collective-permute-start | bytes 393224 | tf_op jit(solution)/shard_map/ppermute | solution.py:131
  14.3 0.5 %shard_map.58 = f32[32,8,128]{2,1,0:T(8,128)S(1)} custom-call(s32[1,1]{1,0:T(1,128)S(6)} %copy.6.count_ref, s32[1,48]{1,0:T(1,128)S(4)} %get-tuple-element.8.rows_ref, s32[1,48]{1,0:T(1,128)S(4)} %get-tuple-element.9.cols_ref, f32[32,8,128]{2,1,0:T(8,128)S(1)} %bitcast.9, f32[1,48,128,128]{3,2,1,0:T(8,128)S(1)} %get-tuple-element.10.tiles_ref), custom_call_target="tpu_custom_call" | custom-call | flops 50331648 | bytes 3145728 | tf_op jit(solution)/shard_map/pallas_call | solution.py:96
  14.9 0.1 collective-permute-start.1
  14.9 0.9 %shard_map.56.parts_ref = bf16[48,128,256]{2,1,0:T(8,128)(2,1)S(1)} custom-call(f32[1,48,128,128]{3,2,1,0:T(8,128)S(1)} %get-tuple-element.10.tiles_ref), custom_call_target="tpu_custom_call" | custom-call | bytes 6291456 | tf_op jit(solution)/shard_map/pallas_call | solution.py:63
  15.8 0.7 %collective-permute-done.seg_ref = f32[32,8,128]{2,1,0:T(8,128)S(1)} collective-permute-done((f32[32,8,128]{2,1,0:T(8,128)S(1)}, f32[32,8,128]{2,1,0:T(8,128)S(1)}, u32[]{:S(2)}, u32[]{:S(2)}) %collective-permute-start) | collective-permute-done | bytes 131104 | tf_op jit(solution)/shard_map/ppermute | solution.py:131
  16.5 0.5 %shard_map.57 = f32[32,8,128]{2,1,0:T(8,128)S(1)} custom-call(s32[1,1]{1,0:T(1,128)S(6)} %copy.6.count_ref, s32[1,48]{1,0:T(1,128)S(4)} %get-tuple-element.8.rows_ref, s32[1,48]{1,0:T(1,128)S(4)} %get-tuple-element.9.cols_ref, f32[32,8,128]{2,1,0:T(8,128)S(1)} %collective-permute-done.seg_ref, bf16[48,128,256]{2,1,0:T(8,128)(2,1)S(1)} %shard_map.56.parts_ref), custom_call_target="tpu_custom_call" | custom-call | flops 50331648 | bytes 3145728 | tf_op jit(solution)/shard_map/pallas_call | solution.py:96
  17.0 2.7 %collective-permute-done.1 = f32[32,8,128]{2,1,0:T(8,128)S(1)} collective-permute-done((f32[32,8,128]{2,1,0:T(8,128)S(1)}, f32[32,8,128]{2,1,0:T(8,128)S(1)}, u32[]{:S(2)}, u32[]{:S(2)}) %collective-permute-start.1) | collective-permute-done | bytes 131104 | tf_op jit(solution)/shard_map/ppermute | solution.py:133
  19.8 15.5 %all_to_all.10 = f32[8,4,8,128]{3,2,1,0:T(8,128)S(1)} all-to-all(f32[8,4,8,128]{3,2,1,0:T(8,128)S(1)} %bitcast.10), channel_id=1, replica_groups=mesh['row'=32,'col'=8] {'col'}, dimensions={0} | all-to-all | bytes 262144 | tf_op jit(solution)/shard_map/all_to_all | solution.py:136
  35.3 0.6 %reduce_sum.9 = f32[4,8,128]{2,1,0:T(8,128)} reduce(f32[8,4,8,128]{3,2,1,0:T(8,128)S(1)} %all_to_all.10, f32[]{:T(128)} %constant.0.clone.1), dimensions={0}, to_apply=%region_0.0 | reduce | flops 28672 | bytes 147460 | tf_op jit(solution)/shard_map/reduce_sum | solution.py:137
  (1 shorter events, 0.0 us)
Async XLA Ops:
  1.4 11.3 %all-to-all-start = ((f32[8,4,8,128]{3,2,1,0:T(8,128)}), f32[8,4,8,128]{3,2,1,0:T(8,128)S(1)}, u32[]{:S(2)}, u32[]{:S(2)}) async-start(f32[8,4,8,128]{3,2,1,0:T(8,128)} %broadcast_in_dim.2), calls=%async_computation | async-start | bytes 262144 | tf_op jit(solution)/shard_map/all_to_all | solution.py:129
  12.7 3.8 %collective-permute-start = (f32[32,8,128]{2,1,0:T(8,128)S(1)}, f32[32,8,128]{2,1,0:T(8,128)S(1)}, u32[]{:S(2)}, u32[]{:S(2)}) collective-permute-start(f32[32,8,128]{2,1,0:T(8,128)S(1)} %bitcast.8), channel_id=1, source_target_pairs={{4,0},{5,9},{2,18},{7,27},{0,36},{1,45},{6,54},{3,63},{12,8},{13,1... | collective-permute-start | bytes 393224 | tf_op jit(solution)/shard_map/ppermute | solution.py:131
  14.9 4.9 %collective-permute-start.1 = (f32[32,8,128]{2,1,0:T(8,128)S(1)}, f32[32,8,128]{2,1,0:T(8,128)S(1)}, u32[]{:S(2)}, u32[]{:S(2)}) collective-permute-start(f32[32,8,128]{2,1,0:T(8,128)S(1)} %shard_map.58), channel_id=1, source_target_pairs={{0,4},{9,5},{18,6},{27,7},{36,0},{45,1},{54,2},{63,3},{8,12},{17,1... | collective-permute-start | bytes 393224 | tf_op jit(solution)/shard_map/ppermute | solution.py:133

commit v7 on v6

--- a/solution.py
+++ b/solution.py
@@ -8,7 +8,7 @@
 from jax.sharding import PartitionSpec as P
 
 TILE = 128
-CHUNKS = 4
+CHUNKS = 1
 SWAPS = (10, 2, 2, 10)
 AXES = ("row", "col")
 SMEM = pl.BlockSpec(memory_space=pltpu.SMEM)

time: 36.3 us -> 36.3 us (level)
  no operation moved by 1% of the time
where the time goes in v7:
time: 36.3 us; the launch traced here: 35.9 us
  blocking collectives  15.5 us (43%)
  starting transfers between devices  7.58 us (21%)
  waiting for transfers between devices  6.26 us (17%)
  Pallas kernels  3.85 us (11%)
  local copies, waits for them, and re-layouts  1.37 us (4%)
  between operations  0.7 us (2%)
  other arithmetic  0.63 us (2%)
    all_to_all x1, blocking collectives, local(): lax.all_to_all(total, 'col', split_axis=0, concat_axis=0, tiled=True)  15.5 us
    all_to_all x1, starting transfers between devices, local(): lax.all_to_all(jnp.broadcast_to(piece[None], (ncol, *piece.shape)), 'col'...  5.86 us
    all_to_all x1, waiting for transfers between devices, local(): lax.all_to_all(jnp.broadcast_to(piece[None], (ncol, *piece.shape)), 'col'...  2.86 us
    ppermute x1, waiting for transfers between devices, local(): home = lax.ppermute(col_part, AXES, backward)  2.72 us
    pallas_call x1, Pallas kernels, stage(): pl.pallas_call(stage_kernel, out_shape=[pltpu.VMEM(tiles.shape, tiles.dty...  1.94 us
    ppermute x1, starting transfers between devices, local(): other_seg = lax.ppermute(own_seg, AXES, onward)  1.63 us
    broadcast_in_dim x1, local copies, waits for them, and re-layouts, local(): jnp.broadcast_to(piece[None], (ncol, *piece.shape))  1.37 us
    pallas_call x2, Pallas kernels, apply_tiles(): pl.pallas_call(kernel, out_shape=jax.ShapeDtypeStruct(seg.shape, jnp.floa...  1.04 us
  transfers between devices with their start and end apart: 3, of which 3 were waited for; matrix products, arithmetic and copies ran while one was open for 0% of the time, Pallas kernels for 11%

profile of v7, /device:TPU:1, one launch (start us, length us, event | category | flops | bytes accessed | tf_op | source)
XLA Modules:
  0.0 35.9 jit_solution(17918581674096834409)
XLA Ops:
  0.0 1.4 %broadcast_in_dim.2 = f32[8,4,8,128]{3,2,1,0:T(8,128)} broadcast(f32[4,8,128]{2,1,0:T(8,128)} %bitcast.11), dimensions={1,2,3} | broadcast | bytes 147456 | tf_op jit(solution)/shard_map/broadcast_in_dim | solution.py:129
  1.4 5.9 %all-to-all-start = ((f32[8,4,8,128]{3,2,1,0:T(8,128)}), f32[8,4,8,128]{3,2,1,0:T(8,128)S(1)}, u32[]{:S(2)}, u32[]{:S(2)}) async-start(f32[8,4,8,128]{3,2,1,0:T(8,128)} %broadcast_in_dim.2), calls=%async_computation | async-start | bytes 262144 | tf_op jit(solution)/shard_map/all_to_all | solution.py:129
  7.9 1.9 %shard_map.55 = (f32[1,48,128,128]{3,2,1,0:T(8,128)S(1)}, s32[1,48]{1,0:T(1,128)S(4)}, s32[1,48]{1,0:T(1,128)S(4)}) custom-call(f32[1,48,128,128]{3,2,1,0:T(8,128)} %refs_0_.1, s32[1,48]{1,0:T(1,128)} %refs_1_.1, s32[1,48]{1,0:T(1,128)} %refs_2_.1), custom_call_target="tpu_custom_call" | custom-call | bytes 3145728 | tf_op jit(solution)/shard_map/pallas_call | solution.py:45
  9.8 2.9 %all-to-all-done = f32[8,4,8,128]{3,2,1,0:T(8,128)S(1)} async-done(((f32[8,4,8,128]{3,2,1,0:T(8,128)}), f32[8,4,8,128]{3,2,1,0:T(8,128)S(1)}, u32[]{:S(2)}, u32[]{:S(2)}) %all-to-all-start) | async-done | bytes 131104 | tf_op jit(solution)/shard_map/all_to_all | solution.py:129
  12.7 1.6 %collective-permute-start = (f32[32,8,128]{2,1,0:T(8,128)S(1)}, f32[32,8,128]{2,1,0:T(8,128)S(1)}, u32[]{:S(2)}, u32[]{:S(2)}) collective-permute-start(f32[32,8,128]{2,1,0:T(8,128)S(1)} %bitcast.8), channel_id=1, source_target_pairs={{4,0},{5,9},{2,18},{7,27},{0,36},{1,45},{6,54},{3,63},{12,8},{13,1... | collective-permute-start | bytes 393224 | tf_op jit(solution)/shard_map/ppermute | solution.py:131
  14.3 0.5 %shard_map.58 = f32[32,8,128]{2,1,0:T(8,128)S(1)} custom-call(s32[1,1]{1,0:T(1,128)S(6)} %copy.6.count_ref, s32[1,48]{1,0:T(1,128)S(4)} %get-tuple-element.8.rows_ref, s32[1,48]{1,0:T(1,128)S(4)} %get-tuple-element.9.cols_ref, f32[32,8,128]{2,1,0:T(8,128)S(1)} %bitcast.9, f32[1,48,128,128]{3,2,1,0:T(8,128)S(1)} %get-tuple-element.10.tiles_ref), custom_call_target="tpu_custom_call" | custom-call | flops 50331648 | bytes 3145728 | tf_op jit(solution)/shard_map/pallas_call | solution.py:96
  14.9 0.1 collective-permute-start.1
  14.9 0.9 %shard_map.56.parts_ref = bf16[48,128,256]{2,1,0:T(8,128)(2,1)S(1)} custom-call(f32[1,48,128,128]{3,2,1,0:T(8,128)S(1)} %get-tuple-element.10.tiles_ref), custom_call_target="tpu_custom_call" | custom-call | bytes 6291456 | tf_op jit(solution)/shard_map/pallas_call | solution.py:63
  15.8 0.7 %collective-permute-done.seg_ref = f32[32,8,128]{2,1,0:T(8,128)S(1)} collective-permute-done((f32[32,8,128]{2,1,0:T(8,128)S(1)}, f32[32,8,128]{2,1,0:T(8,128)S(1)}, u32[]{:S(2)}, u32[]{:S(2)}) %collective-permute-start) | collective-permute-done | bytes 131104 | tf_op jit(solution)/shard_map/ppermute | solution.py:131
  16.5 0.5 %shard_map.57 = f32[32,8,128]{2,1,0:T(8,128)S(1)} custom-call(s32[1,1]{1,0:T(1,128)S(6)} %copy.6.count_ref, s32[1,48]{1,0:T(1,128)S(4)} %get-tuple-element.8.rows_ref, s32[1,48]{1,0:T(1,128)S(4)} %get-tuple-element.9.cols_ref, f32[32,8,128]{2,1,0:T(8,128)S(1)} %collective-permute-done.seg_ref, bf16[48,128,256]{2,1,0:T(8,128)(2,1)S(1)} %shard_map.56.parts_ref), custom_call_target="tpu_custom_call" | custom-call | flops 50331648 | bytes 3145728 | tf_op jit(solution)/shard_map/pallas_call | solution.py:96
  17.0 2.7 %collective-permute-done.1 = f32[32,8,128]{2,1,0:T(8,128)S(1)} collective-permute-done((f32[32,8,128]{2,1,0:T(8,128)S(1)}, f32[32,8,128]{2,1,0:T(8,128)S(1)}, u32[]{:S(2)}, u32[]{:S(2)}) %collective-permute-start.1) | collective-permute-done | bytes 131104 | tf_op jit(solution)/shard_map/ppermute | solution.py:133
  19.8 15.5 %all_to_all.10 = f32[8,4,8,128]{3,2,1,0:T(8,128)S(1)} all-to-all(f32[8,4,8,128]{3,2,1,0:T(8,128)S(1)} %bitcast.10), channel_id=1, replica_groups=mesh['row'=32,'col'=8] {'col'}, dimensions={0} | all-to-all | bytes 262144 | tf_op jit(solution)/shard_map/all_to_all | solution.py:136
  35.3 0.6 %reduce_sum.9 = f32[4,8,128]{2,1,0:T(8,128)} reduce(f32[8,4,8,128]{3,2,1,0:T(8,128)S(1)} %all_to_all.10, f32[]{:T(128)} %constant.0.clone.1), dimensions={0}, to_apply=%region_0.0 | reduce | flops 28672 | bytes 147460 | tf_op jit(solution)/shard_map/reduce_sum | solution.py:137
  (1 shorter events, 0.0 us)
Async XLA Ops:
  1.4 11.3 %all-to-all-start = ((f32[8,4,8,128]{3,2,1,0:T(8,128)}), f32[8,4,8,128]{3,2,1,0:T(8,128)S(1)}, u32[]{:S(2)}, u32[]{:S(2)}) async-start(f32[8,4,8,128]{3,2,1,0:T(8,128)} %broadcast_in_dim.2), calls=%async_computation | async-start | bytes 262144 | tf_op jit(solution)/shard_map/all_to_all | solution.py:129
  12.7 3.8 %collective-permute-start = (f32[32,8,128]{2,1,0:T(8,128)S(1)}, f32[32,8,128]{2,1,0:T(8,128)S(1)}, u32[]{:S(2)}, u32[]{:S(2)}) collective-permute-start(f32[32,8,128]{2,1,0:T(8,128)S(1)} %bitcast.8), channel_id=1, source_target_pairs={{4,0},{5,9},{2,18},{7,27},{0,36},{1,45},{6,54},{3,63},{12,8},{13,1... | collective-permute-start | bytes 393224 | tf_op jit(solution)/shard_map/ppermute | solution.py:131
  14.9 4.9 %collective-permute-start.1 = (f32[32,8,128]{2,1,0:T(8,128)S(1)}, f32[32,8,128]{2,1,0:T(8,128)S(1)}, u32[]{:S(2)}, u32[]{:S(2)}) collective-permute-start(f32[32,8,128]{2,1,0:T(8,128)S(1)} %shard_map.58), channel_id=1, source_target_pairs={{0,4},{9,5},{18,6},{27,7},{36,0},{45,1},{54,2},{63,3},{8,12},{17,1... | collective-permute-start | bytes 393224 | tf_op jit(solution)/shard_map/ppermute | solution.py:133
